TPU v7x, 32 devices: a whole 2x2x4 slice. The times are simulated.
32 devices in a mesh: dp: 32 (over z, y, x, core).
Axes of the slice: x: 2, y: 2, z: 4, core: 2. Of those that a mesh axis runs over, the one named last changes fastest.
Arguments:
- inputs: bfloat16 [32768, 768], P('dp'), may hold values from -6 to 6
- cotangent: bfloat16 [32768, 768], P('dp'), may hold values from -6 to 6
- counts: int32 [32, 3], P('dp'), may hold values from 0 to 4, as said below
- lengths: int32 [32, 8], P('dp'), may hold values from 0 to 512, as said below
- owners: int32 [12], replicated, may hold values from 0 to 31, as said below
- tile_master: float32 [32, 2, 768, 768], P('dp'), may hold values from -1.1547005 to 1.1547005
- tile_first: float32 [32, 2, 768, 768], P('dp'), may hold values from -1.8 to 1.8
- tile_second: float32 [32, 2, 768, 768], P('dp'), may hold values from 0.02 to 0.4
- tile_ema: float32 [32, 2, 768, 768], P('dp'), may hold values from -1.1547005 to 1.1547005
- bias_vals: float32 [10, 768], replicated, may hold values from -1.2 to 1.2
- gain_vals: float32 [2, 768], replicated, may hold values from 0.5 to 1.5
- vector_first: float32 [12, 768], replicated, may hold values from -1.8 to 1.8
- vector_second: float32 [12, 768], replicated, may hold values from 0.02 to 0.4
- vector_ema: float32 [12, 768], replicated, may hold values from -3 to 3
Outputs:
- mixed: bfloat16 [32768, 768], P('dp')
- input_grad: float32 [32768, 768], P('dp')
- tile_weight: float32 [32, 2, 768, 768], P('dp')
- tile_first_new: float32 [32, 2, 768, 768], P('dp')
- tile_second_new: float32 [32, 2, 768, 768], P('dp')
- tile_ema_new: float32 [32, 2, 768, 768], P('dp')
- tile_copy: bfloat16 [32, 2, 768, 768], P('dp')
- vector_weight: float32 [12, 768], replicated
- vector_first_new: float32 [12, 768], replicated
- vector_second_new: float32 [12, 768], replicated
- vector_ema_new: float32 [12, 768], replicated
Inputs may be any that keep to these rules, and one draw needn't show every extreme that they name: counts[d] gives device d's passages of 512, 256 and 128 slots; every device has one or more of the first kind, and its passages take half of its 1024 slots or more; on some device the counts are 1, 0 and 4. lengths[d, p] is the length of device d's passage p, passages in the order of the counts; each from a quarter of its passage's slots to all of them, 0 past the last passage; each device's first passage is full. owners[t] is the device that holds tile t; no device holds more than 2 tiles, and some device holds 2.
All inputs are finite; a program needn't handle non-finite values.
Results may differ from a plain program's by a relative error of at most 0.014.
The roundings to bfloat16 on the way count: a program that leaves them out, or rounds other values in their place, can miss the bound.
Values may be sent and summed in bfloat16 or wider, within the bound.
A program may use at most 192 MiB of HBM per device.

v0:
```python
import functools

import jax
import jax.numpy as jnp
from jax import lax
from jax.experimental import pallas as pl
from jax.experimental.pallas import tpu as pltpu
from jax.sharding import PartitionSpec as P

HEADS = 12
BUCKET = 128
SLOTS = 2
TILES = 12
VROWS = 12
STEP = 5

norm_epsilon = 1e-12
tile_rate = 0.03
vector_rate = 0.2
first_decay = 0.5
second_decay = 0.5
adam_epsilon = 1e-08
weight_decay = 0.01
average_rate = 0.9


def tile_slots(owners):
    order = jnp.arange(owners.shape[0], dtype=jnp.int32)
    same = owners[:, None] == owners[None, :]
    earlier = order[None, :] < order[:, None]
    return jnp.sum((same & earlier).astype(jnp.int32), 1)


def adam_update(param, grad, first, second, rate):
    first_new = first_decay * first + (1.0 - first_decay) * grad
    second_new = second_decay * second + (1.0 - second_decay) * grad * grad
    first_hat = first_new / (1.0 - first_decay**STEP)
    second_hat = second_new / (1.0 - second_decay**STEP)
    param_new = param - rate * (
        first_hat / (jnp.sqrt(second_hat) + adam_epsilon) + weight_decay * param
    )
    return (param_new, first_new, second_new)


ROWS = 4 * BUCKET
TAIL_RATE = 0.28
TAIL_SERIES = (
    0.11615256574707405,
    0.06981038475559553,
    0.2631359597579608,
    -0.22983675561378278,
    0.38546775012288165,
    -0.10472989053809521,
)
INV_SQRT_TAU = 0.3989422804014327
ALLOWED = 3.0e38
BARRED = -1000000000.0


def dot(left, right):
    return jnp.dot(left, right, preferred_element_type=jnp.float32)


def dot_back(left, right):
    return lax.dot_general(
        left, right, (((1,), (1,)), ((), ())), preferred_element_type=jnp.float32
    )


def outer(left, right):
    return lax.dot_general(
        left, right, (((0,), (0,)), ((), ())), preferred_element_type=jnp.float32
    )


def passage_facts(counts, lengths, position):
    places = lengths.shape[1]
    big_end = counts[0, 0]
    mid_end = big_end + counts[0, 1]
    all_end = mid_end + counts[0, 2]
    start = jnp.int32(0)
    member = jnp.zeros(position.shape, jnp.int32)
    usable = jnp.zeros(position.shape, jnp.int32)
    for number in range(places):
        size = jnp.where(
            number < big_end,
            4 * BUCKET,
            jnp.where(number < mid_end, 2 * BUCKET, jnp.where(number < all_end, BUCKET, 0)),
        )
        inside = (position >= start) & (position < start + size)
        live = inside & (position < start + lengths[0, number])
        member = jnp.where(inside, number + 1, member)
        usable = jnp.where(live, 1, usable)
        start = start + size
    passage = jnp.where(member > 0, member - 1, places + position // BUCKET)
    return usable, passage


def normalize(values):
    center = jnp.mean(values, -1, keepdims=True)
    centered = values - center
    spread = jnp.mean(centered * centered, -1, keepdims=True)
    inverse = lax.rsqrt(spread + norm_epsilon)
    return centered * inverse, inverse


def normalize_back(grad, hat, inverse):
    center = jnp.mean(grad, -1, keepdims=True)
    along = jnp.mean(grad * hat, -1, keepdims=True)
    return inverse * (grad - center - hat * along)


def columns_total(values):
    return jnp.sum(values, 0, keepdims=True)


def attention_caps(counts, lengths, block):
    at_row = lax.broadcasted_iota(jnp.int32, (ROWS, 1), 0) + block * ROWS
    at_column = lax.broadcasted_iota(jnp.int32, (1, ROWS), 1) + block * ROWS
    _, passage_row = passage_facts(counts, lengths, at_row)
    usable_column, passage_column = passage_facts(counts, lengths, at_column)
    allowed = (passage_row == passage_column) & ((usable_column == 1) | (at_row == at_column))
    return jnp.where(allowed, ALLOWED, BARRED)


def attend_quad(quad, weight, x_ref, vec_ref, cap_ref, q_ref, k_ref, v_ref, p_ref, ctx_ref):
    cols = pl.ds(pl.multiple_of(quad * 256, 256), 256)
    x = x_ref[...]
    query = (dot(x, weight(0, cols)) + vec_ref[0:1, cols]).astype(jnp.bfloat16)
    query = query * jnp.bfloat16(0.125)
    keyed = dot(x, weight(1, cols)).astype(jnp.bfloat16)
    valued = (dot(x, weight(2, cols)) + vec_ref[1:2, cols]).astype(jnp.bfloat16)
    q_ref[...] = query
    k_ref[...] = keyed
    v_ref[...] = valued
    low_half = lax.broadcasted_iota(jnp.int32, (1, 128), 1) < 64
    for pair in range(2):
        part = slice(128 * pair, 128 * pair + 128)
        contexts = []
        for head in range(2):
            here = low_half if head == 0 else ~low_half
            mine = jnp.where(here, query[:, part], jnp.zeros_like(query[:, part]))
            scores = jnp.minimum(dot_back(mine, keyed[:, part]), cap_ref[...])
            exponent = jnp.exp(scores - jnp.max(scores, -1, keepdims=True))
            inverse = 1.0 / jnp.sum(exponent, -1, keepdims=True)
            probability = (exponent * inverse).astype(jnp.bfloat16)
            p_ref[0, 2 * pair + head] = probability
            contexts.append(dot(probability, valued[:, part]))
        both = jnp.where(low_half, contexts[0], contexts[1]).astype(jnp.bfloat16)
        ctx_ref[:, pl.ds(pl.multiple_of(quad * 256 + 128 * pair, 128), 128)] = both


def close_block(w_out, x_ref, vec_ref, ctx_ref, hat_ref, inverse_ref):
    branch = dot(ctx_ref[...], w_out) + vec_ref[2:3, :]
    hat_ref[...], inverse_ref[...] = normalize(x_ref[...].astype(jnp.float32) + branch)


def attend_back_pair(pull, level_from, p_ref, query, keyed, valued):
    low_half = lax.broadcasted_iota(jnp.int32, (1, 128), 1) < 64
    along = pull.astype(jnp.float32) * level_from.astype(jnp.float32)
    by_query, by_key, by_value = [], [], []
    for head in range(2):
        mask = low_half if head == 0 else ~low_half
        mine = jnp.where(mask, pull, jnp.zeros_like(pull))
        level = jnp.sum(jnp.where(mask, along, 0.0), -1, keepdims=True)
        probability = p_ref[head]
        grad_prob = dot_back(mine, valued)
        grad_scores = (probability.astype(jnp.float32) * (grad_prob - level)).astype(jnp.bfloat16)
        by_query.append(dot(grad_scores, keyed))
        by_key.append(outer(grad_scores, query))
        by_value.append(outer(probability, pull))
    grad_query = jnp.where(low_half, by_query[0], by_query[1]) * 0.125
    grad_key = jnp.where(low_half, by_key[0], by_key[1])
    grad_value = jnp.where(low_half, by_value[0], by_value[1])
    return [value.astype(jnp.bfloat16) for value in (grad_query, grad_key, grad_value)]


def gelu_parts(up):
    near = 1.0 / (1.0 + TAIL_RATE * jnp.abs(up))
    decay = jnp.exp(up * up * -0.5)
    series = jnp.full_like(near, TAIL_SERIES[-1])
    for term in TAIL_SERIES[-2::-1]:
        series = series * near + term
    tail = series * near * decay
    share = jnp.where(up < 0.0, tail, 1.0 - tail)
    slope = share + up * (decay * INV_SQRT_TAU)
    return (up * share).astype(jnp.bfloat16), slope


def attend_forward(
    counts,
    lengths,
    x_ref,
    w_hbm,
    vec_ref,
    q_ref,
    k_ref,
    v_ref,
    p_ref,
    ctx_ref,
    hat_ref,
    inverse_ref,
    w_buf,
    cap_ref,
    w_sem,
):
    block, quad = pl.program_id(0), pl.program_id(1)
    loads = [pltpu.make_async_copy(w_hbm.at[at], w_buf.at[at], w_sem.at[at]) for at in range(4)]

    @pl.when((block == 0) & (quad == 0))
    def _():
        for load in loads:
            load.start()
        for load in loads:
            load.wait()

    @pl.when(quad == 0)
    def _():
        cap_ref[...] = attention_caps(counts, lengths, block)

    def weight(at, cols):
        return w_buf[at, :, cols]

    attend_quad(quad, weight, x_ref, vec_ref, cap_ref, q_ref, k_ref, v_ref, p_ref, ctx_ref)

    @pl.when(quad == 2)
    def _():
        close_block(w_buf[3], x_ref, vec_ref, ctx_ref, hat_ref, inverse_ref)


def attended(counts, lengths, x, weights, vectors):
    tokens, width = x.shape
    blocks = tokens // ROWS
    low = jnp.bfloat16
    smem = pl.BlockSpec(memory_space=pltpu.SMEM)
    quad = pl.BlockSpec((ROWS, 256), lambda b, h: (b, h))
    rows = pl.BlockSpec((ROWS, width), lambda b, h: (b, 0))
    shaped = jax.ShapeDtypeStruct
    return pl.pallas_call(
        attend_forward,
        grid=(blocks, 3),
        out_shape=(
            shaped((tokens, width), low),
            shaped((tokens, width), low),
            shaped((tokens, width), low),
            shaped((blocks, HEADS, ROWS, ROWS), low),
            shaped((tokens, width), low),
            shaped((tokens, width), jnp.float32),
            shaped((tokens, 1), jnp.float32),
        ),
        in_specs=[
            smem,
            smem,
            rows,
            pl.BlockSpec(memory_space=pl.ANY),
            pl.BlockSpec((VROWS, width), lambda b, h: (0, 0)),
        ],
        out_specs=(
            quad,
            quad,
            quad,
            pl.BlockSpec((1, 4, ROWS, ROWS), lambda b, h: (b, h, 0, 0)),
            rows,
            rows,
            pl.BlockSpec((ROWS, 1), lambda b, h: (b, 0)),
        ),
        scratch_shapes=[
            pltpu.VMEM((4, width, width), low),
            pltpu.VMEM((ROWS, ROWS), jnp.float32),
            pltpu.SemaphoreType.DMA((4,)),
        ],
        compiler_params=pltpu.CompilerParams(vmem_limit_bytes=56 * 2**20),
        name="attend_forward",
    )(counts, lengths, x, weights, vectors)


def feed_forward_both(
    counts,
    lengths,
    hat_ref,
    inverse_ref,
    cot_ref,
    w_hbm,
    vec_ref,
    mixed_ref,
    first_ref,
    branch_ref,
    context_ref,
    up_grad_ref,
    down_grad_ref,
    sum_ref,
    w_buf,
    active_ref,
    up_ref,
    hidden_ref,
    down_ref,
    slope_ref,
    w_sem,
):
    step = pl.program_id(0)
    blocks = pl.num_programs(0) - 4
    loads = [
        pltpu.make_async_copy(w_hbm.at[3 + at], w_buf.at[at], w_sem.at[at]) for at in range(9)
    ]

    @pl.when(step == 0)
    def _():
        for load in loads[1:] + loads[:1]:
            load.start()
        sum_ref[...] = jnp.zeros_like(sum_ref)
        for load in loads[1:] + loads[:1]:
            load.wait()

    @pl.when(step < blocks)
    def _():
        here = pl.ds(pl.multiple_of(step * ROWS, ROWS), ROWS)
        at_row = lax.broadcasted_iota(jnp.int32, (ROWS, 1), 0) + step * ROWS
        live = passage_facts(counts, lengths, at_row)[0].astype(jnp.float32)
        hat = hat_ref[...]
        hidden = hat * vec_ref[10:11, :] + vec_ref[8:9, :]
        hidden_low = hidden.astype(jnp.bfloat16)
        hidden_ref[here, :] = hidden_low
        total = hidden + vec_ref[7:8, :]
        for tile in range(4):
            up = dot(hidden_low, w_buf[1 + tile]) + vec_ref[3 + tile : 4 + tile, :]
            active, slope = gelu_parts(up)
            slope_ref[tile] = slope.astype(jnp.bfloat16)
            active_ref[tile, here, :] = active
            total = total + dot(active, w_buf[5 + tile])
        hat_two, inverse_two = normalize(total)
        mixed_ref[...] = ((hat_two * vec_ref[11:12, :] + vec_ref[9:10, :]) * live).astype(jnp.bfloat16)
        grad_out = cot_ref[...].astype(jnp.float32) * live
        sum_ref[11:12, :] += columns_total(grad_out * hat_two)
        sum_ref[9:10, :] += columns_total(grad_out)
        second = normalize_back(grad_out * vec_ref[11:12, :], hat_two, inverse_two)
        down_low = second.astype(jnp.bfloat16)
        down_ref[here, :] = down_low
        sum_ref[7:8, :] += columns_total(down_low.astype(jnp.float32))
        grad_hidden = second
        for tile in range(4):
            pulled = dot_back(down_low, w_buf[5 + tile])
            up_low = (pulled * slope_ref[tile].astype(jnp.float32)).astype(jnp.bfloat16)
            up_ref[tile, here, :] = up_low
            sum_ref[3 + tile : 4 + tile, :] += columns_total(up_low.astype(jnp.float32))
            grad_hidden = grad_hidden + dot_back(up_low, w_buf[1 + tile])
        sum_ref[10:11, :] += columns_total(grad_hidden * hat)
        sum_ref[8:9, :] += columns_total(grad_hidden)
        grad_first = normalize_back(grad_hidden * vec_ref[10:11, :], hat, inverse_ref[...])
        first_ref[...] = grad_first
        branch_low = grad_first.astype(jnp.bfloat16)
        branch_ref[...] = branch_low
        sum_ref[2:3, :] += columns_total(branch_low.astype(jnp.float32))
        context_ref[...] = dot_back(branch_low, w_buf[0]).astype(jnp.bfloat16)

    @pl.when(step >= blocks)
    def _():
        tile = step - blocks
        up_grad_ref[0] = outer(hidden_ref[...], up_ref[tile]).astype(jnp.bfloat16)
        down_grad_ref[0] = outer(active_ref[tile], down_ref[...]).astype(jnp.bfloat16)


def fed_forward_both(counts, lengths, hat, inverse, cotangent, weights, vectors):
    tokens, width = hat.shape
    blocks = tokens // ROWS
    low = jnp.bfloat16
    smem = pl.BlockSpec(memory_space=pltpu.SMEM)
    shaped = jax.ShapeDtypeStruct

    def block_of(step):
        return jnp.minimum(step, blocks - 1)

    def tile_of(step):
        return jnp.maximum(step - blocks, 0)

    rows = pl.BlockSpec((ROWS, width), lambda i: (block_of(i), 0))
    tile = pl.BlockSpec((1, width, width), lambda i: (tile_of(i), 0, 0))
    return pl.pallas_call(
        feed_forward_both,
        grid=(blocks + 4,),
        out_shape=(
            shaped((tokens, width), low),
            shaped((tokens, width), jnp.float32),
            shaped((tokens, width), low),
            shaped((tokens, width), low),
            shaped((4, width, width), low),
            shaped((4, width, width), low),
            shaped((16, width), jnp.float32),
        ),
        in_specs=[
            smem,
            smem,
            rows,
            pl.BlockSpec((ROWS, 1), lambda i: (block_of(i), 0)),
            rows,
            pl.BlockSpec(memory_space=pl.ANY),
            pl.BlockSpec((VROWS, width), lambda i: (0, 0)),
        ],
        out_specs=(
            rows,
            rows,
            rows,
            rows,
            tile,
            tile,
            pl.BlockSpec((16, width), lambda i: (0, 0)),
        ),
        scratch_shapes=[
            pltpu.VMEM((9, width, width), low),
            pltpu.VMEM((4, tokens, width), low),
            pltpu.VMEM((4, tokens, width), low),
            pltpu.VMEM((tokens, width), low),
            pltpu.VMEM((tokens, width), low),
            pltpu.VMEM((4, ROWS, width), low),
            pltpu.SemaphoreType.DMA((9,)),
        ],
        compiler_params=pltpu.CompilerParams(vmem_limit_bytes=60 * 2**20),
        name="feed_forward_both",
    )(counts, lengths, hat, inverse, cotangent, weights, vectors)


def attend_backward(
    p_ref,
    q_ref,
    k_ref,
    v_ref,
    x_ref,
    ctx_ref,
    grad_ctx_ref,
    branch_ref,
    first_ref,
    w_ref,
    input_ref,
    grad_ref,
    sum_ref,
    pulled,
):
    step = pl.program_id(0)
    quad, block = step // 2, lax.rem(step, 2)
    here = pl.ds(pl.multiple_of(block * ROWS, ROWS), ROWS)
    cols = pl.ds(pl.multiple_of(quad * 256, 256), 256)

    @pl.when(step == 0)
    def _():
        sum_ref[...] = jnp.zeros_like(sum_ref)
        input_ref[...] = first_ref[...]

    for pair in range(2):
        half = slice(128 * pair, 128 * pair + 128)
        at = pl.ds(pl.multiple_of(quad * 256 + 128 * pair, 128), 128)
        heads = p_ref.at[0, pl.ds(2 * pair, 2)]
        grads = attend_back_pair(
            grad_ctx_ref[here, at], ctx_ref[here, at], heads, q_ref[:, half], k_ref[:, half], v_ref[:, half]
        )
        for number, grad in enumerate(grads):
            pulled[number, here, half] = grad
        sum_ref[0:1, at] += columns_total(grads[0].astype(jnp.float32))
        sum_ref[1:2, at] += columns_total(grads[2].astype(jnp.float32))

    more = input_ref[here, :]
    for at in range(3):
        more = more + dot_back(pulled[at, here, :], w_ref[at, :, cols])
    input_ref[here, :] = more

    @pl.when(block == 1)
    def _():
        for tile in range(3):
            grad_ref[tile, :, cols] = outer(x_ref[...], pulled[tile]).astype(jnp.bfloat16)
        grad_ref[3, :, cols] = outer(ctx_ref[...], branch_ref[:, cols]).astype(jnp.bfloat16)


def attended_back(probs, query, keyed, valued, x, context, grad_context, grad_branch, grad_first, weights):
    tokens, width = x.shape
    low = jnp.bfloat16
    shaped = jax.ShapeDtypeStruct
    once = pl.Buffered(1)
    quad = pl.BlockSpec((ROWS, 256), lambda i: (lax.rem(i, 2), i // 2))
    whole = pl.BlockSpec((tokens, width), lambda i: (0, 0), pipeline_mode=once)
    return pl.pallas_call(
        attend_backward,
        grid=(6,),
        out_shape=(
            shaped((tokens, width), jnp.float32),
            shaped((4, width, width), low),
            shaped((16, width), jnp.float32),
        ),
        in_specs=[
            pl.BlockSpec((1, 4, ROWS, ROWS), lambda i: (lax.rem(i, 2), i // 2, 0, 0)),
            quad,
            quad,
            quad,
            whole,
            whole,
            whole,
            whole,
            whole,
            pl.BlockSpec((3, width, width), lambda i: (0, 0, 0), pipeline_mode=once),
        ],
        out_specs=(
            whole,
            pl.BlockSpec((4, width, width), lambda i: (0, 0, 0), pipeline_mode=once),
            pl.BlockSpec((16, width), lambda i: (0, 0)),
        ),
        scratch_shapes=[pltpu.VMEM((3, tokens, 256), low)],
        compiler_params=pltpu.CompilerParams(vmem_limit_bytes=56 * 2**20),
        name="attend_backward",
    )(probs, query, keyed, valued, x, context, grad_context, grad_branch, grad_first, weights)


def moved(param, grad, first, second, average, rate):
    param_new, first_new, second_new = adam_update(param, grad, first, second, rate)
    return param_new, first_new, second_new, average_rate * average + (1.0 - average_rate) * param_new


def update_kernel(
    gain_scale,
    grad_ref,
    master_ref,
    first_ref,
    second_ref,
    ema_ref,
    vec_grad_ref,
    bias_ref,
    gain_ref,
    vec_first_ref,
    vec_second_ref,
    vec_ema_ref,
    mixed_in,
    input_in,
    master_out,
    first_out,
    second_out,
    ema_out,
    copy_out,
    vec_out,
    vec_first_out,
    vec_second_out,
    vec_ema_out,
    mixed_out,
    input_out,
    vec_ref,
):
    mixed_out[...] = mixed_in[...]
    input_out[...] = input_in[...]

    @pl.when((pl.program_id(0) == 0) & (pl.program_id(1) == 0))
    def _():
        vec_ref[0:10, :] = bias_ref[...]
        vec_ref[10:12, :] = gain_ref[...]
        vec_grad = vec_grad_ref[0:VROWS, :] * gain_scale
        vec_out[...], vec_first_out[...], vec_second_out[...], vec_ema_out[...] = moved(
            vec_ref[...], vec_grad, vec_first_ref[...], vec_second_ref[...], vec_ema_ref[...], vector_rate
        )

    grad = grad_ref[...].astype(jnp.float32) * gain_scale
    result = moved(master_ref[0], grad, first_ref[0], second_ref[0], ema_ref[0], tile_rate)
    master_out[0], first_out[0], second_out[0], ema_out[0] = result
    copy_out[0] = result[0].astype(jnp.bfloat16)


def updated(
    gain_scale,
    slot_grads,
    master,
    first,
    second,
    ema,
    vec_grad,
    bias,
    gain,
    vec_first,
    vec_second,
    vec_ema,
    mixed,
    input_grad,
):
    width = master.shape[-1]
    chunk = 192
    tile = pl.BlockSpec((1, 1, chunk, width), lambda s, r: (0, s, r, 0))
    steps = width // chunk
    rows = pl.BlockSpec((mixed.shape[0] // (SLOTS * steps), width), lambda s, r: (s * steps + r, 0))

    def whole(value):
        return pl.BlockSpec(value.shape, lambda s, r: (0, 0))

    shaped = jax.ShapeDtypeStruct
    tile_shape = shaped(master.shape, jnp.float32)
    vec_shape = shaped((VROWS, width), jnp.float32)
    results = pl.pallas_call(
        functools.partial(update_kernel, gain_scale),
        grid=(SLOTS, steps),
        out_shape=(tile_shape,) * 4
        + (shaped(master.shape, jnp.bfloat16),)
        + (vec_shape,) * 4
        + (shaped(mixed.shape, mixed.dtype), shaped(input_grad.shape, input_grad.dtype)),
        in_specs=[pl.BlockSpec((1, chunk, width), lambda s, r: (s, r, 0))]
        + [tile] * 4
        + [whole(value) for value in (vec_grad, bias, gain, vec_first, vec_second, vec_ema)]
        + [rows] * 2,
        out_specs=(tile,) * 5 + (whole(vec_first),) * 4 + (rows,) * 2,
        scratch_shapes=[pltpu.VMEM((VROWS, width), jnp.float32)],
        compiler_params=pltpu.CompilerParams(vmem_limit_bytes=62 * 2**20),
        name="update",
    )(
        slot_grads,
        master,
        first,
        second,
        ema,
        vec_grad,
        bias,
        gain,
        vec_first,
        vec_second,
        vec_ema,
        mixed,
        input_grad,
    )
    return results[-2:] + results[:-2]


MESH = pl.DeviceIdType.MESH
GROUP = 32
PAIRS = TILES // 2
PLANE = 8
PIECE = 96
PAIR_TILES = ((0, 1), (2, 3), (4, 8), (5, 9), (6, 10), (7, 11))


def remote(src, dst, send, recv, device):
    return pltpu.make_async_remote_copy(
        src_ref=src, dst_ref=dst, send_sem=send, recv_sem=recv, device_id=(device,), device_id_type=MESH
    )


def place(device):
    core = lax.rem(device, 2)
    x = lax.rem(device // 2, 2)
    y = lax.rem(device // 4, 2)
    z = device // 8
    return z, y, x, core


def start(copies):
    for copy in copies:
        copy.start()


def arrive(copies):
    for copy in copies:
        copy.wait_recv()


def greet(z, in_plane):
    barrier = pltpu.get_barrier_semaphore()
    for hop in range(1, PLANE):
        other = z * PLANE + lax.rem(in_plane + hop, PLANE)
        pl.semaphore_signal(barrier, inc=1, device_id=(other,), device_id_type=MESH)
    for hop in range(1, 4):
        other = lax.rem(z + hop, 4) * PLANE + in_plane
        pl.semaphore_signal(barrier, inc=1, device_id=(other,), device_id_type=MESH)
    pl.semaphore_wait(barrier, PLANE + 2)


def along_z(z, in_plane):
    inner = (1 + z // 2) * PLANE + in_plane
    other_middle = (3 - z) * PLANE + in_plane
    outer_end = lax.rem(lax.rem(z + 3, 4) * 3, 4) * PLANE + in_plane
    return inner, other_middle, outer_end


def third(part):
    return pl.ds(256 * part, 256)


UNITS = [(0, 4, pl.ds(256 * part, 256)) for part in range(3)]
UNITS += [(2 * pair, 2, pl.ds(0, 768)) for pair in range(2, PAIRS)]
Z_PARTS = (pl.ds(0, 512), pl.ds(512, 256))


POSITIONS = [tile for pair in PAIR_TILES for tile in pair]


def slot_number(owners, tile):
    number = jnp.int32(0)
    for earlier in range(tile):
        number = number + jnp.where(owners[earlier] == owners[tile], 1, 0)
    return number

FRONT_PLAN = (
    (
        ("open",),
        ("swap", 0),
        ("sent", 0),
        ("swap", 1),
        ("choose", 0),
        ("end", 0),
        ("sent", 1),
        ("swap", 2),
        ("middle", 0),
        ("choose", 1),
        ("end", 1),
        ("caps",),
        ("middle", 1),
        ("total", 0),
        ("end", 3, 0),
        ("choose", 2),
        ("end", 3, 1),
        ("end", 2),
        ("end", 4, 0),
        ("mid", 0),
        ("far", 0),
        ("end", 5, 0),
        ("middle", 3, 0),
        ("total", 1),
        ("near", 0),
        ("end", 4, 1),
        ("middle", 3, 1),
        ("total", 3, 0),
        ("mid", 1),
        ("total", 3, 1),
        ("middle", 2),
        ("end", 5, 1),
        ("mid", 3),
        ("finish", 0),
        ("end", 6, 0),
        ("far", 1),
    ),
    (
        ("middle", 4, 0),
        ("total", 2),
        ("far", 3),
        ("near", 1),
        ("middle", 4, 1),
        ("mid", 2),
        ("middle", 5, 0),
        ("total", 4, 0),
    ),
    (
        ("middle", 5, 1),
        ("total", 4, 1),
        ("end", 6, 1),
        ("mid", 4),
        ("finish", 1),
    ),
    (
        ("middle", 6, 0),
        ("total", 5, 1),
        ("far", 2),
        ("total", 5, 0),
        ("near", 3),
    ),
    (
        ("middle", 6, 1),
        ("far", 4),
        ("total", 6, 0),
        ("total", 6, 1),
        ("near", 2),
        ("mid", 5),
        ("finish", 3),
        ("keep", 2),
        ("finish", 2),
        ("keep", 0),
        ("keep", 1),
        ("mid", 6),
    ),
    (
        ("far", 5),
    ),
    (
        ("far", 6),
        ("near", 4),
    ),
    (
        ("finish", 4),
        ("keep", 3),
        ("near", 5),
    ),
    (
        ("near", 6),
        ("finish", 5),
        ("keep", 4),
    ),
    (
        ("finish", 6),
        ("keep", 5),
    ),
)


def gather_and_forward(
    counts,
    lengths,
    owners,
    bias_ref,
    gain_ref,
    x_hbm,
    cot_hbm,
    master_hbm,
    q_ref,
    k_ref,
    v_ref,
    p_ref,
    ctx_hbm,
    x_turned_hbm,
    ctx_turned_hbm,
    hidden_hbm,
    active_hbm,
    slope_hbm,
    down_hbm,
    mixed_hbm,
    second_hbm,
    hat_hbm,
    w_out,
    inverse_ref,
    sum_ref,
    vec_ref,
    cap_ref,
    wide,
    low,
    stage_a,
    stage_b,
    stage_c,
    chosen,
    from_end,
    from_middle,
    w_buf,
    x_then_hidden,
    x_turned,
    ctx_turned,
    hidden_turned,
    ctx_ref,
    cot_then_down,
    mixed_ref,
    hat_ref,
    slope_buf,
    active_buf,
    load_sem,
    store_sem,
    tile_sem,
    out_sem,
    swap_send,
    swap_recv,
    z_send,
    z_recv,
    mid_send,
    mid_recv,
    far_send,
    far_recv,
    near_send,
    near_recv,
):
    step = pl.program_id(0)
    width = 8 * PIECE
    me = lax.axis_index("dp")
    z, y, x, core = place(me)
    in_plane = lax.rem(me, PLANE)
    sibling = me + 1 - 2 * core
    x_peer = me + 2 - 4 * x
    y_peer = me + 4 - 8 * y
    z_targets = along_z(z, in_plane)
    stages = (stage_a, stage_b, stage_c)
    is_end = (z == 0) | (z == 3)
    is_middle = (z == 1) | (z == 2)

    def piece_rows(cell_core, cell_x, cell_y):
        return pl.ds(pl.multiple_of(((cell_core * 2 + cell_x) * 2 + cell_y) * PIECE, 16), PIECE)

    def swap(part):
        def send(hop, carry):
            target = lax.rem(in_plane + hop, PLANE)
            _, ty, tx, tc = place(target)
            remote(
                low.at[:, piece_rows(tc, tx, ty), third(part)],
                stages[part].at[pl.ds(2 * in_plane, 2)],
                swap_send.at[part],
                swap_recv.at[part],
                z * PLANE + target,
            ).start()
            return carry

        lax.fori_loop(1, PLANE, send, 0)

    def swap_wait(part, sem):
        most = stages[part].at[pl.ds(0, 2 * PLANE - 2)]
        pltpu.make_async_copy(most, most, sem.at[part]).wait()

    def z_copy(unit, part, level):
        first, count, cols = UNITS[unit]
        tiles = pl.ds(first, count)
        cols = cols if count == 4 else Z_PARTS[part]
        src = w_buf.at[tiles, core, x, y, :, cols] if level == 2 else chosen.at[tiles, :, cols]
        dst = (from_end.at[tiles, :, cols], from_middle.at[tiles, :, cols], src)[level]
        at = level, unit, part
        return remote(src, dst, z_send.at[at], z_recv.at[at], z_targets[level])

    def z_parts(unit):
        return range(1 if UNITS[unit][1] == 4 else 2)

    def z_end(unit, part=0):
        @pl.when(is_end)
        def _():
            z_copy(unit, part, 0).start()

    def z_rows(unit, part):
        first, count, cols = UNITS[unit]
        return pl.ds(first, count), cols if count == 4 else Z_PARTS[part]

    def z_middle(unit, part=0):
        @pl.when(is_middle)
        def _():
            z_copy(unit, part, 0).wait_recv()
            tiles, cols = z_rows(unit, part)
            chosen[tiles, :, cols] = chosen[tiles, :, cols] + from_end[tiles, :, cols]
            z_copy(unit, part, 1).start()

    def z_total(unit, part=0):
        @pl.when(is_middle)
        def _():
            z_copy(unit, part, 1).wait_recv()
            tiles, cols = z_rows(unit, part)
            w_buf[tiles, core, x, y, :, cols] = chosen[tiles, :, cols] + from_middle[tiles, :, cols]
            z_copy(unit, part, 2).start()

    def mid_copies(unit):
        first, count, cols = UNITS[unit]
        copies = []
        for n, peer in enumerate((y_peer, x_peer)):
            spot = w_buf.at[pl.ds(first + n * count // 2, count // 2), core, x, y, :, cols]
            copies.append(remote(spot, spot, mid_send.at[unit, n], mid_recv.at[unit, n], peer))
        return copies

    def far_copies(unit):
        first, count, cols = UNITS[unit]
        half = count // 2
        by_row = w_buf.at[pl.ds(first, half), core, x, :, :, cols]
        by_column = w_buf.at[pl.ds(first + half, half), core, :, y, :, cols]
        return [
            remote(spot, spot, far_send.at[unit, n], far_recv.at[unit, n], peer)
            for n, (spot, peer) in enumerate(((by_row, x_peer), (by_column, y_peer)))
        ]

    def near_copy(unit):
        first, count, cols = UNITS[unit]
        spot = w_buf.at[pl.ds(first, count), core, :, :, :, cols]
        return remote(spot, spot, near_send.at[unit], near_recv.at[unit], sibling)

    def give_mid(unit):
        @pl.when(is_end)
        def _():
            arrive([z_copy(unit, part, 2) for part in z_parts(unit)])

        start(mid_copies(unit))

    def give_far(unit):
        arrive(mid_copies(unit))
        start(far_copies(unit))

    def give_near(unit):
        arrive(far_copies(unit))
        near_copy(unit).start()

    def finish(unit):
        near_copy(unit).wait_recv()

    def choose(part):
        swap_wait(part, swap_recv)
        for pair in range(PAIRS):
            for n, tile in enumerate(PAIR_TILES[pair]):
                owner = owners[tile]
                value = stages[part][SLOTS * lax.rem(owner, PLANE) + slot_number(owners, tile)]
                chosen[2 * pair + n, :, third(part)] = jnp.where(
                    owner // PLANE == z, value, jnp.zeros_like(value)
                )

    def load(at):
        src = (x_hbm, cot_hbm, master_hbm)[at]
        dst = (x_then_hidden, cot_then_down, wide)[at]
        return pltpu.make_async_copy(src, dst, load_sem.at[at])

    def store(at):
        src, dst = (
            (hidden_turned, hidden_hbm),
            (ctx_ref, ctx_hbm),
            (hat_ref, hat_hbm),
            (cot_then_down, down_hbm),
            (mixed_ref, mixed_hbm),
            (wide, second_hbm),
            (x_turned, x_turned_hbm),
            (ctx_turned, ctx_turned_hbm),
        )[at]
        src = src.at[pl.ds(0, 2 * ROWS)] if src is wide else src
        return pltpu.make_async_copy(src, dst, store_sem.at[at])

    def w_store(pair):
        two = pl.ds(2 * pair, 2)
        return pltpu.make_async_copy(w_buf.at[two], w_out.at[two], out_sem.at[pair])

    def weight(at, cols=slice(None)):
        value = w_buf[at, :, :, :, :, cols]
        return value.reshape(width, value.shape[-1])

    def open_all():
        for at in range(3):
            load(at).start()
        sum_ref[...] = jnp.zeros_like(sum_ref)
        vec_ref[0:10, :] = bias_ref[...]
        vec_ref[10:12, :] = gain_ref[...]
        greet(z, in_plane)
        load(2).wait()
        for slot in range(SLOTS):
            low[slot] = wide[width * slot : width * (slot + 1), :].astype(jnp.bfloat16)
        for part in range(3):
            stages[part][pl.ds(2 * in_plane, 2)] = low[:, piece_rows(core, x, y), third(part)]

    def make_caps():
        for block in range(2):
            cap_ref[block] = attention_caps(counts, lengths, block)
        load(0).wait()
        x_turned[...] = x_then_hidden[...].T
        store(6).start()
        load(1).wait()

    actions = {
        "open": open_all,
        "caps": make_caps,
        "swap": swap,
        "sent": lambda part: swap_wait(part, swap_send),
        "choose": choose,
        "end": z_end,
        "middle": z_middle,
        "total": z_total,
        "mid": give_mid,
        "far": give_far,
        "near": give_near,
        "finish": finish,
        "keep": lambda pair: w_store(pair).start(),
    }

    for at, work in enumerate(FRONT_PLAN):

        @pl.when(step == at)
        def _():
            for name, *rest in work:
                actions[name](*rest)

    quad, block = step // 2, lax.rem(step, 2)
    here = pl.ds(pl.multiple_of(block * ROWS, ROWS), ROWS)

    @pl.when(step < 6)
    def _():
        attend_quad(
            quad,
            weight,
            x_then_hidden.at[here],
            vec_ref,
            cap_ref.at[block],
            q_ref,
            k_ref,
            v_ref,
            p_ref,
            ctx_ref.at[here],
        )

    @pl.when((step >= 4) & (step < 6))
    def _():
        branch = dot(ctx_ref[here, :], weight(3)) + vec_ref[2:3, :]
        hat, inverse = normalize(x_then_hidden[here, :].astype(jnp.float32) + branch)
        hat_ref[here, :] = hat.astype(jnp.bfloat16)
        inverse_ref[here, :] = inverse
        hidden = hat * vec_ref[10:11, :] + vec_ref[8:9, :]
        hidden_low = hidden.astype(jnp.bfloat16)
        x_then_hidden[here, :] = hidden_low
        hidden_turned[:, here] = hidden_low.T
        ctx_turned[:, here] = ctx_ref[here, :].T
        wide[here, :] = hidden + vec_ref[7:8, :]

    @pl.when(step == 5)
    def _():
        start([store(0), store(1), store(2), store(7)])

    turn = step - 6
    slot = lax.rem(turn, 2)

    def tile_stores(source_slot, tile):
        return [
            pltpu.make_async_copy(src.at[source_slot], dst.at[tile], tile_sem.at[source_slot, at])
            for at, (src, dst) in enumerate(((active_buf, active_hbm), (slope_buf, slope_hbm)))
        ]

    @pl.when(turn >= 2)
    def _():
        for copy in tile_stores(slot, 0):
            copy.wait()

    @pl.when(turn >= 0)
    def _():
        for half in range(2):
            rows = slice(ROWS * half, ROWS * half + ROWS)
            up = dot(x_then_hidden[rows, :], weight(4 + 2 * turn)) + vec_ref[pl.ds(3 + turn, 1), :]
            active, slope = gelu_parts(up)
            slope_buf[slot, rows, :] = slope.astype(jnp.bfloat16)
            active_buf[slot, :, rows] = active.T
            wide[rows, :] = wide[rows, :] + dot(active, weight(5 + 2 * turn))
        start(tile_stores(slot, turn))

    @pl.when(step == 9)
    def _():
        for half in range(2):
            rows = slice(ROWS * half, ROWS * half + ROWS)
            at_row = lax.broadcasted_iota(jnp.int32, (ROWS, 1), 0) + half * ROWS
            live = passage_facts(counts, lengths, at_row)[0].astype(jnp.float32)
            hat, inverse = normalize(wide[rows, :])
            mixed = (hat * vec_ref[11:12, :] + vec_ref[9:10, :]) * live
            mixed_ref[rows, :] = mixed.astype(jnp.bfloat16)
            grad_out = cot_then_down[rows, :].astype(jnp.float32) * live
            sum_ref[11:12, :] += columns_total(grad_out * hat)
            sum_ref[9:10, :] += columns_total(grad_out)
            second = normalize_back(grad_out * vec_ref[11:12, :], hat, inverse)
            wide[rows, :] = second
            down_low = second.astype(jnp.bfloat16)
            cot_then_down[rows, :] = down_low
            sum_ref[7:8, :] += columns_total(down_low.astype(jnp.float32))
        start([store(3), store(4), store(5)])
        for at in range(2):
            for copy in tile_stores(at, 0):
                copy.wait()
        for pair in range(PAIRS):
            w_store(pair).wait()
        swap_wait(2, swap_send)
        for unit in range(len(UNITS)):
            for copy in mid_copies(unit) + far_copies(unit) + [near_copy(unit)]:
                copy.wait_send()

            @pl.when(is_end)
            def _():
                for part in z_parts(unit):
                    z_copy(unit, part, 0).wait_send()

            @pl.when(is_middle)
            def _():
                for part in z_parts(unit):
                    z_copy(unit, part, 1).wait_send()
                    z_copy(unit, part, 2).wait_send()

        for at in range(8):
            store(at).wait()


def gathered_and_forwarded(counts, lengths, owners, bias, gain, x, cotangent, master):
    tokens, width = x.shape
    blocks = tokens // ROWS
    low, high = jnp.bfloat16, jnp.float32
    smem = pl.BlockSpec(memory_space=pltpu.SMEM)
    any_space = pl.BlockSpec(memory_space=pl.ANY)
    dma = pltpu.SemaphoreType.DMA
    shaped = jax.ShapeDtypeStruct

    def at(step):
        step = jnp.minimum(step, 5)
        return lax.rem(step, 2), step // 2

    quad = pl.BlockSpec((ROWS, 256), at)
    rows = shaped((tokens, width), low)
    turned = shaped((width, tokens), low)
    cut = (2, 2, 2, PIECE, width)
    units = len(UNITS)
    return pl.pallas_call(
        gather_and_forward,
        grid=(10,),
        out_shape=(
            rows,
            rows,
            rows,
            shaped((blocks, HEADS, ROWS, ROWS), low),
            rows,
            turned,
            turned,
            turned,
            shaped((4, width, tokens), low),
            shaped((4, tokens, width), low),
            rows,
            rows,
            shaped((tokens, width), high),
            rows,
            shaped((TILES,) + cut, low),
            shaped((tokens, 1), high),
            shaped((16, width), high),
        ),
        in_specs=[smem] * 3
        + [pl.BlockSpec(bias.shape, lambda i: (0, 0)), pl.BlockSpec(gain.shape, lambda i: (0, 0))]
        + [any_space] * 3,
        out_specs=(quad, quad, quad, pl.BlockSpec((1, 4, ROWS, ROWS), lambda i: (*at(i), 0, 0)))
        + (any_space,) * 11
        + (
            pl.BlockSpec((tokens, 1), lambda i: (0, 0), pipeline_mode=pl.Buffered(1)),
            pl.BlockSpec((16, width), lambda i: (0, 0)),
        ),
        scratch_shapes=[
            pltpu.VMEM((VROWS, width), high),
            pltpu.VMEM((2, ROWS, ROWS), high),
            pltpu.VMEM((SLOTS * width, width), high),
            pltpu.VMEM((SLOTS, width, width), low),
            pltpu.VMEM((2 * PLANE, PIECE, 256), low),
            pltpu.VMEM((2 * PLANE, PIECE, 256), low),
            pltpu.VMEM((2 * PLANE, PIECE, 256), low),
            pltpu.VMEM((TILES, PIECE, width), low),
            pltpu.VMEM((TILES, PIECE, width), low),
            pltpu.VMEM((TILES, PIECE, width), low),
            pltpu.VMEM((TILES,) + cut, low),
            pltpu.VMEM((tokens, width), low),
            pltpu.VMEM((width, tokens), low),
            pltpu.VMEM((width, tokens), low),
            pltpu.VMEM((width, tokens), low),
            pltpu.VMEM((tokens, width), low),
            pltpu.VMEM((tokens, width), low),
            pltpu.VMEM((tokens, width), low),
            pltpu.VMEM((tokens, width), low),
            pltpu.VMEM((2, tokens, width), low),
            pltpu.VMEM((2, width, tokens), low),
            dma((3,)),
            dma((8,)),
            dma((2, 2)),
            dma((PAIRS,)),
            dma((3,)),
            dma((3,)),
            dma((3, units, 2)),
            dma((3, units, 2)),
            dma((units, 2)),
            dma((units, 2)),
            dma((units, 2)),
            dma((units, 2)),
            dma((units,)),
            dma((units,)),
        ],
        compiler_params=pltpu.CompilerParams(
            collective_id=0, has_side_effects=True, vmem_limit_bytes=63 * 2**20
        ),
        name="gather_and_forward",
    )(counts, lengths, owners, bias, gain, x, cotangent, master.reshape(SLOTS * width, width))


BACK_PLAN = (
    (),
    (),
    (
        ("core", 0),
    ),
    (),
    (
        ("far", 0),
        ("core", 1),
    ),
    (),
    (
        ("far", 1),
        ("core", 2),
        ("mid", 0),
    ),
    (
        ("far", 2),
    ),
    (
        ("end", 0),
    ),
    (
        ("mid", 1),
        ("core", 3),
    ),
    (),
    (
        ("mid", 2),
        ("far", 3),
        ("end", 1),
        ("middle", 0),
    ),
    (),
    (),
    (
        ("middle", 1),
        ("core", 4),
        ("end", 2),
        ("total", 0),
        ("mid", 3),
    ),
    (
        ("far", 4),
    ),
    (
        ("middle", 2),
        ("end", 3),
        ("core", 5),
        ("total", 1),
    ),
    (
        ("mid", 4),
    ),
    (
        ("far", 5),
        ("end", 4),
        ("middle", 3),
        ("total", 2),
    ),
    (),
    (
        ("core", 6),
        ("total", 3),
        ("middle", 4),
        ("take", 0),
        ("mid", 5),
        ("take", 1),
        ("sum", 0),
        ("take", 2),
        ("far", 6),
        ("total", 4),
        ("end", 5),
        ("middle", 5),
        ("mid", 6),
        ("sum", 1),
        ("end", 6),
        ("take", 3),
        ("take", 4),
        ("deliver", 0),
        ("total", 5),
        ("middle", 6),
        ("sum", 2),
        ("take", 5),
        ("deliver", 1),
        ("total", 6),
        ("take", 6),
        ("deliver", 2),
        ("input", 0),
        ("input", 1),
    ),
)


def backward_and_reduce(
    owners,
    p_ref,
    q_ref,
    k_ref,
    v_ref,
    ctx_ref,
    inverse_ref,
    gain_ref,
    late_ref,
    x_turned_hbm,
    ctx_turned_hbm,
    hidden_hbm,
    active_hbm,
    slope_hbm,
    down_hbm,
    second_hbm,
    hat_hbm,
    w_hbm,
    input_hbm,
    slot_grad,
    vec_out,
    w_part,
    acc,
    hidden_then_x,
    active_then_ctx,
    down_then_branch,
    grad_ctx_ref,
    hat_ref,
    slope_then_query,
    up_then_key,
    value_buf,
    part,
    from_core,
    from_far,
    from_mid,
    from_end,
    from_middle,
    total,
    snap,
    outbox,
    vec_now,
    vec_in,
    holds,
    keeps,
    load_sem,
    w_sem,
    core_send,
    core_recv,
    far_send,
    far_recv,
    mid_send,
    mid_recv,
    z_send,
    z_recv,
    vec_send,
    vec_recv,
    out_send,
    out_recv,
):
    step = pl.program_id(0)
    inner = jnp.maximum(step - 4, 0)
    quad, block, pair = inner // 4, lax.rem(inner, 4) // 2, lax.rem(inner, 2)
    me = lax.axis_index("dp")
    z, y, x, core = place(me)
    in_plane = lax.rem(me, PLANE)
    sibling = me + 1 - 2 * core
    x_peer = me + 2 - 4 * x
    y_peer = me + 4 - 8 * y
    z_targets = along_z(z, in_plane)
    is_end = (z == 0) | (z == 3)
    is_middle = (z == 1) | (z == 2)

    def tiles_of(batch):
        if batch < 4:
            return w_part, 4 + 2 * batch, 2, slice(None)
        return part, 0, 4, pl.ds(256 * (batch - 4), 256)

    def halves(batch, turned):
        ref, first, count, cols = tiles_of(batch)
        return ref, pl.ds(first + turned * count // 2, count // 2), cols

    def core_copy(batch):
        ref, first, count, cols = tiles_of(batch)
        tiles = pl.ds(first, count)
        return remote(
            ref.at[tiles, 1 - core, :, :, :, cols],
            from_core.at[tiles, :, :, :, cols],
            core_send.at[batch],
            core_recv.at[batch],
            sibling,
        )

    def far_copies(batch):
        copies = []
        for turned in range(2):
            ref, tiles, cols = halves(batch, turned)
            src = ref.at[tiles, core, :, 1 - y, :, cols] if turned else ref.at[tiles, core, 1 - x, :, :, cols]
            copies.append(
                remote(
                    src,
                    from_far.at[tiles, :, :, cols],
                    far_send.at[batch, turned],
                    far_recv.at[batch, turned],
                    y_peer if turned else x_peer,
                )
            )
        return copies

    def mid_copies(batch):
        copies = []
        for turned in range(2):
            ref, tiles, cols = halves(batch, turned)
            src = ref.at[tiles, core, 1 - x, y, :, cols] if turned else ref.at[tiles, core, x, 1 - y, :, cols]
            copies.append(
                remote(
                    src,
                    from_mid.at[tiles, :, cols],
                    mid_send.at[batch, turned],
                    mid_recv.at[batch, turned],
                    x_peer if turned else y_peer,
                )
            )
        return copies

    def z_copy(batch, stage):
        ref, first, count, cols = tiles_of(batch)
        tiles = pl.ds(first, count)
        if stage == 2:
            src, dst = total.at[tiles, :, cols], total.at[tiles, :, cols]
        else:
            src = ref.at[tiles, core, x, y, :, cols]
            dst = (from_middle if stage else from_end).at[tiles, :, cols]
        return remote(src, dst, z_send.at[stage, batch], z_recv.at[stage, batch], z_targets[stage])

    def give_core(batch):
        core_copy(batch).start()

    def give_far(batch):
        core_copy(batch).wait_recv()
        ref, first, count, cols = tiles_of(batch)
        for tile in range(first, first + count):
            ref[tile, core, :, :, :, cols] = ref[tile, core, :, :, :, cols] + from_core[tile, :, :, :, cols]
        start(far_copies(batch))

    def give_mid(batch):
        arrive(far_copies(batch))
        for turned in range(2):
            ref, tiles, cols = halves(batch, turned)
            if turned:
                ref[tiles, core, :, y, :, cols] = ref[tiles, core, :, y, :, cols] + from_far[tiles, :, :, cols]
            else:
                ref[tiles, core, x, :, :, cols] = ref[tiles, core, x, :, :, cols] + from_far[tiles, :, :, cols]
        start(mid_copies(batch))

    def add_piece(batch, other):
        ref, first, count, cols = tiles_of(batch)
        tiles = pl.ds(first, count)
        return ref[tiles, core, x, y, :, cols] + other[tiles, :, cols]

    def give_end(batch):
        arrive(mid_copies(batch))
        ref, first, count, cols = tiles_of(batch)
        ref[pl.ds(first, count), core, x, y, :, cols] = add_piece(batch, from_mid)

        @pl.when(is_end)
        def _():
            z_copy(batch, 0).start()

    def give_middle(batch):
        @pl.when(is_middle)
        def _():
            z_copy(batch, 0).wait_recv()
            ref, first, count, cols = tiles_of(batch)
            ref[pl.ds(first, count), core, x, y, :, cols] = add_piece(batch, from_end)
            z_copy(batch, 1).start()

    def give_total(batch):
        @pl.when(is_middle)
        def _():
            z_copy(batch, 1).wait_recv()
            _, first, count, cols = tiles_of(batch)
            total[pl.ds(first, count), :, cols] = add_piece(batch, from_middle)
            z_copy(batch, 2).start()

    def take_total(batch):
        @pl.when(is_end)
        def _():
            z_copy(batch, 2).wait_recv()

    def deliver(third):
        cols = pl.ds(256 * third, 256)
        snap[...] = total[:, :, cols]

        def fill(at, carry):
            value = snap[holds[at]]
            outbox[third, at] = jnp.where(keeps[at] > 0, value, jnp.zeros_like(value))
            return carry

        lax.fori_loop(0, 2 * PLANE, fill, 0)

        def send(hop, carry):
            target = lax.rem(in_plane + hop, PLANE)
            remote(
                outbox.at[third, pl.ds(2 * target, 2)],
                slot_grad.at[:, core, x, y, :, cols],
                out_send.at[third],
                out_recv.at[third],
                z * PLANE + target,
            ).start()
            return carry

        lax.fori_loop(1, PLANE, send, 0)
        keep_copy(third).start()

    def keep_copy(third):
        return pltpu.make_async_copy(
            outbox.at[third, pl.ds(2 * in_plane, 2)],
            slot_grad.at[:, core, x, y, :, pl.ds(256 * third, 256)],
            load_sem.at[5 + third],
        )

    def vec_copies(stage):
        if stage < 3:
            hops = [(stage, (sibling, x_peer, y_peer)[stage])]
        else:
            hops = [
                (2 + hop, lax.rem(z + hop, 4) * PLANE + in_plane) for hop in range(1, 4)
            ]
        return [
            remote(vec_now.at[stage], vec_in.at[at], vec_send.at[at], vec_recv.at[at], device)
            for at, device in hops
        ]

    def vec_next(stage):
        arrive(vec_copies(stage))
        vec_now[stage + 1] = vec_now[stage] + vec_in[stage]
        start(vec_copies(stage + 1))

    def input_store():
        return pltpu.make_async_copy(acc, input_hbm, load_sem.at[4])

    def load(at):
        src, dst = (
            (hidden_hbm, hidden_then_x),
            (down_hbm, down_then_branch),
            (second_hbm, acc),
            (hat_hbm, hat_ref),
            None,
            None,
            None,
            None,
            (x_turned_hbm, hidden_then_x),
            (ctx_turned_hbm, active_then_ctx),
        )[at]
        return pltpu.make_async_copy(src, dst, load_sem.at[at])

    def tile_load(tile, side):
        src, dst = ((slope_hbm, slope_then_query), (active_hbm, active_then_ctx))[side]
        return pltpu.make_async_copy(src.at[tile], dst, load_sem.at[10 + side])

    def w_load(at):
        return pltpu.make_async_copy(w_hbm.at[at], w_part.at[at], w_sem.at[at])

    def weight(at, cols=slice(None)):
        value = w_part[at, :, :, :, :, cols]
        return value.reshape(8 * PIECE, value.shape[-1])

    def input_rows(half):
        rows = slice(ROWS * half, ROWS * half + ROWS)
        more = acc[rows, :]
        for at, buf in enumerate((slope_then_query, up_then_key, value_buf)):
            more = more + dot_back(buf[rows, :], weight(at))
        acc[rows, :] = more
        if half == 1:
            input_store().start()

    actions = {
        "core": give_core,
        "far": give_far,
        "mid": give_mid,
        "end": give_end,
        "middle": give_middle,
        "total": give_total,
        "take": take_total,
        "deliver": deliver,
        "sum": vec_next,
        "input": input_rows,
    }

    @pl.when(step == 0)
    def _():
        start([load(1), tile_load(0, 0), w_load(5), w_load(4), load(2), tile_load(0, 1), load(0)])
        start([w_load(at) for at in range(6, TILES)] + [load(3)] + [w_load(3 - at) for at in range(4)])
        for at in range(2 * PLANE):
            tile_here, kept = jnp.int32(0), jnp.int32(0)
            for tile in range(TILES):
                place_of = SLOTS * owners[tile] + slot_number(owners, tile)
                match = place_of == z * 2 * PLANE + at
                tile_here = tile_here + jnp.where(match, POSITIONS.index(tile), 0)
                kept = kept + jnp.where(match, 1, 0)
            holds[at] = tile_here
            keeps[at] = kept
        vec_now[0] = late_ref[...]
        greet(z, in_plane)

    def serve(points):
        for at in points:
            if BACK_PLAN[at]:

                @pl.when(step == (at // 2 if at < 8 else at - 4))
                def _():
                    for name, number in BACK_PLAN[at]:
                        actions[name](number)

    serve(range(0, 8, 2))

    @pl.when(step < 4)
    def _():
        tile_load(step, 0).wait()
        w_load(5 + 2 * step).wait()

        @pl.when(step == 0)
        def _():
            load(1).wait()

        for half in range(2):
            rows = slice(ROWS * half, ROWS * half + ROWS)
            back = dot_back(down_then_branch[rows, :], weight(5 + 2 * step))
            up_low = (back * slope_then_query[rows, :].astype(jnp.float32)).astype(jnp.bfloat16)
            up_then_key[rows, :] = up_low
            vec_now[0, pl.ds(3 + step, 1), :] += columns_total(up_low.astype(jnp.float32))

        @pl.when(step < 3)
        def _():
            tile_load(step + 1, 0).start()

        w_load(4 + 2 * step).wait()

        @pl.when(step == 0)
        def _():
            load(2).wait()
            load(0).wait()

        for half in range(2):
            rows = slice(ROWS * half, ROWS * half + ROWS)
            acc[rows, :] = acc[rows, :] + dot_back(up_then_key[rows, :], weight(4 + 2 * step))

    serve(range(1, 8, 2))

    @pl.when(step < 4)
    def _():
        tile_load(step, 1).wait()
        by_down = dot(active_then_ctx[...], down_then_branch[...]).astype(jnp.bfloat16)
        w_part[5 + 2 * step] = by_down.reshape(2, 2, 2, PIECE, 8 * PIECE)

        @pl.when(step < 3)
        def _():
            tile_load(step + 1, 1).start()

        by_up = dot(hidden_then_x[...], up_then_key[...]).astype(jnp.bfloat16)
        w_part[4 + 2 * step] = by_up.reshape(2, 2, 2, PIECE, 8 * PIECE)

    @pl.when(step == 3)
    def _():
        start([load(8), load(9)])
        load(3).wait()
        for at in range(4):
            w_load(at).wait()
        for half in range(2):
            rows = slice(ROWS * half, ROWS * half + ROWS)
            grad_hidden, hat = acc[rows, :], hat_ref[rows, :].astype(jnp.float32)
            vec_now[0, 10:11, :] += columns_total(grad_hidden * hat)
            vec_now[0, 8:9, :] += columns_total(grad_hidden)
            first = normalize_back(grad_hidden * gain_ref[0:1, :], hat, inverse_ref[rows, :])
            acc[rows, :] = first
            branch_low = first.astype(jnp.bfloat16)
            down_then_branch[rows, :] = branch_low
            vec_now[0, 2:3, :] += columns_total(branch_low.astype(jnp.float32))
            grad_ctx_ref[rows, :] = dot_back(branch_low, weight(3)).astype(jnp.bfloat16)

    serve(range(8, 20))

    here = pl.ds(pl.multiple_of(block * ROWS, ROWS), ROWS)
    quad_cols = pl.ds(pl.multiple_of(quad * 256, 256), 256)

    pair_cols = pl.ds(pl.multiple_of(quad * 256 + pair * 128, 128), 128)
    grad_bufs = (slope_then_query, up_then_key, value_buf)

    @pl.when(step >= 4)
    def _():
        grads = attend_back_pair(
            grad_ctx_ref[here, pair_cols],
            ctx_ref[here, pair_cols],
            p_ref.at[0],
            q_ref[...],
            k_ref[...],
            v_ref[...],
        )
        for buf, grad in zip(grad_bufs, grads):
            buf[here, pair_cols] = grad
        vec_now[0, 0:1, pair_cols] += columns_total(grads[0].astype(jnp.float32))
        vec_now[0, 1:2, pair_cols] += columns_total(grads[2].astype(jnp.float32))

    @pl.when(step == 7)
    def _():
        load(8).wait()
        load(9).wait()

    @pl.when((step >= 4) & (block == 1) & (pair == 1))
    def _():
        for tile in range(4):
            if tile < 3:
                value = dot(hidden_then_x[...], grad_bufs[tile][:, quad_cols])
            else:
                value = dot(active_then_ctx[...], down_then_branch[:, quad_cols])
            value = value.astype(jnp.bfloat16).reshape(2, 2, 2, PIECE, 256)
            part[tile, :, :, :, :, quad_cols] = value


    @pl.when(step == 15)
    def _():
        start(vec_copies(0))
        for name, number in BACK_PLAN[-1]:
            actions[name](number)
        arrive(vec_copies(3))
        summed = jnp.zeros(vec_out.shape, jnp.float32)
        for origin in range(4):
            hop = lax.rem(z - origin + 4, 4)
            summed = summed + jnp.where(hop == 0, vec_now[3], vec_in[2 + jnp.maximum(hop, 1)])
        vec_out[...] = summed
        for batch in range(7):
            for copy in [core_copy(batch)] + far_copies(batch) + mid_copies(batch):
                copy.wait_send()

            @pl.when(is_end)
            def _():
                z_copy(batch, 0).wait_send()

            @pl.when(is_middle)
            def _():
                z_copy(batch, 1).wait_send()
                z_copy(batch, 2).wait_send()

        for stage in range(4):
            for copy in vec_copies(stage):
                copy.wait_send()
        input_store().wait()
        for third in range(3):
            keep_copy(third).wait()
            most = outbox.at[third, pl.ds(0, 2 * PLANE - 2)]
            pltpu.make_async_copy(most, most, out_recv.at[third]).wait()
            pltpu.make_async_copy(most, most, out_send.at[third]).wait()


def backward_and_reduced(
    owners,
    probs,
    query,
    keyed,
    valued,
    context,
    inverse,
    gain,
    late_sums,
    x_turned,
    ctx_turned,
    hidden,
    active,
    slope,
    grad_down,
    grad_second,
    hat,
    weights,
):
    tokens, width = grad_down.shape
    low, high = jnp.bfloat16, jnp.float32
    shaped = jax.ShapeDtypeStruct
    smem = pl.BlockSpec(memory_space=pltpu.SMEM)
    any_space = pl.BlockSpec(memory_space=pl.ANY)
    dma = pltpu.SemaphoreType.DMA
    once = pl.Buffered(1)

    def at(step):
        inner = jnp.maximum(step - 4, 0)
        return lax.rem(inner, 4) // 2, inner // 4 * 2 + lax.rem(inner, 2)

    pair = pl.BlockSpec((ROWS, 128), at)
    sums = pl.BlockSpec((16, width), lambda i: (0, 0))
    cut = (2, 2, 2, PIECE, width)
    input_grad, slot_grads, vector_sums = pl.pallas_call(
        backward_and_reduce,
        grid=(16,),
        out_shape=(
            shaped((tokens, width), high),
            shaped((SLOTS,) + cut, low),
            shaped((16, width), high),
        ),
        in_specs=[smem, pl.BlockSpec((1, 2, ROWS, ROWS), lambda i: (*at(i), 0, 0))]
        + [pair] * 3
        + [
            pl.BlockSpec((tokens, width), lambda i: (0, 0), pipeline_mode=once),
            pl.BlockSpec((tokens, 1), lambda i: (0, 0), pipeline_mode=once),
            pl.BlockSpec(gain.shape, lambda i: (0, 0)),
            sums,
        ]
        + [any_space] * 9,
        out_specs=(any_space, any_space, sums),
        scratch_shapes=[
            pltpu.VMEM((TILES,) + cut, low),
            pltpu.VMEM((tokens, width), high),
            pltpu.VMEM((width, tokens), low),
            pltpu.VMEM((width, tokens), low),
            pltpu.VMEM((tokens, width), low),
            pltpu.VMEM((tokens, width), low),
            pltpu.VMEM((tokens, width), low),
            pltpu.VMEM((tokens, width), low),
            pltpu.VMEM((tokens, width), low),
            pltpu.VMEM((tokens, width), low),
            pltpu.VMEM((4,) + cut, low),
            pltpu.VMEM((TILES,) + cut[1:], low),
            pltpu.VMEM((TILES,) + cut[2:], low),
            pltpu.VMEM((TILES,) + cut[3:], low),
            pltpu.VMEM((TILES,) + cut[3:], low),
            pltpu.VMEM((TILES,) + cut[3:], low),
            pltpu.VMEM((TILES,) + cut[3:], low),
            pltpu.VMEM((TILES, PIECE, 256), low),
            pltpu.VMEM((3, 2 * PLANE, PIECE, 256), low),
            pltpu.VMEM((4, 16, width), high),
            pltpu.VMEM((6, 16, width), high),
            pltpu.SMEM((2 * PLANE,), jnp.int32),
            pltpu.SMEM((2 * PLANE,), jnp.int32),
            dma((12,)),
            dma((TILES,)),
            dma((7,)),
            dma((7,)),
            dma((7, 2)),
            dma((7, 2)),
            dma((7, 2)),
            dma((7, 2)),
            dma((3, 7)),
            dma((3, 7)),
            dma((6,)),
            dma((6,)),
            dma((3,)),
            dma((3,)),
        ],
        compiler_params=pltpu.CompilerParams(
            collective_id=1, has_side_effects=True, vmem_limit_bytes=63 * 2**20
        ),
        name="backward_and_reduce",
    )(
        owners,
        probs,
        query,
        keyed,
        valued,
        context,
        inverse,
        gain,
        late_sums,
        x_turned,
        ctx_turned,
        hidden,
        active,
        slope,
        grad_down,
        grad_second,
        hat,
        weights,
    )
    return input_grad, slot_grads.reshape(SLOTS, width, width), vector_sums


def collected_tiles(tile_low, owners, slots):
    mine = owners == lax.axis_index("dp")
    local = jnp.where(mine[:, None, None], tile_low[slots], jnp.zeros((), tile_low.dtype))
    return lax.psum(local, "dp")


def summed_over_slice(parts, vector_terms, owners, slots):
    myself = lax.axis_index("dp")

    def add(held, items):
        part, owner, slot = items
        total = lax.psum(part.astype(jnp.float32), "dp")
        here = (owner == myself) & (slot == jnp.arange(SLOTS, dtype=jnp.int32))
        return held + jnp.where(here[:, None, None], total[None], 0.0), None

    empty = jnp.zeros((SLOTS,) + parts.shape[1:], jnp.float32)
    return lax.scan(add, empty, (parts, owners, slots))[0], lax.psum(vector_terms, "dp")


def body(
    inputs,
    cotangent,
    counts,
    lengths,
    owners,
    tile_master,
    tile_first,
    tile_second,
    tile_ema,
    bias_vals,
    gain_vals,
    vector_first,
    vector_second,
    vector_ema,
):
    tokens = inputs.shape[0]
    small = lax.axis_size("dp") == GROUP
    gain_scale = float(tokens * lax.axis_size("dp")) ** (-0.5)
    if small:
        (
            query,
            keyed,
            valued,
            probs,
            context,
            x_turned,
            ctx_turned,
            hidden,
            active,
            slope,
            grad_down,
            mixed,
            grad_second,
            hat,
            weights,
            inverse,
            late_sums,
        ) = gathered_and_forwarded(
            counts,
            lengths,
            owners,
            bias_vals,
            gain_vals,
            inputs,
            cotangent,
            tile_master,
        )
        input_grad, slot_grads, full_sums = backward_and_reduced(
            owners,
            probs,
            query,
            keyed,
            valued,
            context,
            inverse,
            gain_vals,
            late_sums,
            x_turned,
            ctx_turned,
            hidden,
            active,
            slope,
            grad_down,
            grad_second,
            hat,
            weights,
        )
    else:
        slots = tile_slots(owners)
        vectors = jnp.concatenate([bias_vals, gain_vals], 0)
        weights = collected_tiles(tile_master[0].astype(jnp.bfloat16), owners, slots)
        query, keyed, valued, probs, context, hat, inverse = attended(
            counts, lengths, inputs, weights, vectors
        )
        mixed, grad_first, grad_branch, grad_context, up_grads, down_grads, late_sums = fed_forward_both(
            counts, lengths, hat, inverse, cotangent, weights, vectors
        )
        input_grad, early_grads, early_sums = attended_back(
            probs, query, keyed, valued, inputs, context, grad_context, grad_branch, grad_first, weights
        )
        parts = jnp.concatenate([early_grads, up_grads, down_grads], 0)
        slot_grads, full_sums = summed_over_slice(parts, late_sums + early_sums, owners, slots)
    return updated(
        gain_scale,
        slot_grads,
        tile_master,
        tile_first,
        tile_second,
        tile_ema,
        full_sums,
        bias_vals,
        gain_vals,
        vector_first,
        vector_second,
        vector_ema,
        mixed,
        input_grad,
    )


def solution(mesh):
    placed = (
        P("dp", None),
        P("dp", None),
        P("dp", None),
        P("dp", None),
        P(),
        P("dp", None, None, None),
        P("dp", None, None, None),
        P("dp", None, None, None),
        P("dp", None, None, None),
        P(),
        P(),
        P(),
        P(),
        P(),
    )
    return jax.shard_map(
        body,
        mesh=mesh,
        in_specs=placed,
        out_specs=(
            P("dp", None),
            P("dp", None),
            P("dp", None, None, None),
            P("dp", None, None, None),
            P("dp", None, None, None),
            P("dp", None, None, None),
            P("dp", None, None, None),
            P(),
            P(),
            P(),
            P(),
        ),
        check_vma=False,
    )
```

profile of v0, /device:TPU:11, one launch (start us, length us, event | category | flops | bytes accessed | tf_op | source)
XLA Modules:
  0.0 255.4 jit_solution(788583605904801698)
XLA Ops:
  0.6 113.9 %gather_and_forward.1 = (bf16[1024,768]{1,0:T(8,128)(2,1)}, bf16[1024,768]{1,0:T(8,128)(2,1)}, bf16[1024,768]{1,0:T(8,128)(2,1)}, bf16[2,12,512,512]{3,2,1,0:T(8...) custom-call(s32[1,3]{1,0:T(1,128)} %counts.1, ...), custom_call_target="tpu_custom_call" | custom-call | tf_op jit(solution)/shard_map/gather_and_forward/pallas_call | solution.py:1167
  114.5 121.1 %backward_and_reduce.1 = (f32[1024,768]{1,0:T(8,128)}, bf16[2,2,2,2,96,768]{5,4,3,2,1,0:T(8,128)(2,1)}, f32[16,768]{1,0:T(8,128)}) custom-call(s32[12]{0:T(128)} %owners.3, bf16[2,12,512,512]{3,2,1,0:T(8,128)(2,1)} %get-tuple-element.42.p_ref, bf16[1024,768]{1,0:T(8,128)(2,1)} %get-tuple-element.43.q_ref, bf16[1024,768]{1,0:T(8,128)(2,1)} %get-tuple-element.44.k_ref, ...), custom_call_target="tpu_custom_call" | custom-call | tf_op jit(solution)/shard_map/backward_and_reduce/pallas_call | solution.py:1827
  235.6 19.7 %update.1 = (f32[1,2,768,768]{3,2,1,0:T(8,128)}, f32[1,2,768,768]{3,2,1,0:T(8,128)}, f32[1,2,768,768]{3,2,1,0:T(8,128)}, f32[1,2,768,768]{3,2,1,0:T(8,128)}, bf1...) custom-call(bf16[2,768,768]{2,1,0:T(8,128)(2,1)} %bitcast.3, ...), custom_call_target="tpu_custom_call" | custom-call | tf_op jit(solution)/shard_map/update/pallas_call | solution.py:588
where the time goes:
time: 257 us; the launch traced here: 255 us
  Pallas kernels  255 us (99%)
    pallas_call x1, Pallas kernels, backward_and_reduced(): pl.pallas_call(backward_and_reduce, grid=(16,), out_shape=(shaped((tokens...  121 us
    pallas_call x1, Pallas kernels, gathered_and_forwarded(): pl.pallas_call(gather_and_forward, grid=(10,), out_shape=(rows, rows, row...  114 us
    pallas_call x1, Pallas kernels, updated(): pl.pallas_call(functools.partial(update_kernel, gain_scale), grid=(SLOTS,...  19.7 us

commit v1 on v0

--- a/solution.py
+++ b/solution.py
@@ -574,7 +574,7 @@
     input_grad,
 ):
     width = master.shape[-1]
-    chunk = 192
+    chunk = 96
     tile = pl.BlockSpec((1, 1, chunk, width), lambda s, r: (0, s, r, 0))
     steps = width // chunk
     rows = pl.BlockSpec((mixed.shape[0] // (SLOTS * steps), width), lambda s, r: (s * steps + r, 0))
@@ -695,84 +695,84 @@
         ("choose", 0),
         ("end", 0),
         ("sent", 1),
-        ("swap", 2),
         ("middle", 0),
         ("choose", 1),
         ("end", 1),
-        ("caps",),
-        ("middle", 1),
+        ("swap", 2),
         ("total", 0),
         ("end", 3, 0),
+        ("middle", 1),
+        ("mid", 0),
         ("choose", 2),
+        ("end", 2),
         ("end", 3, 1),
-        ("end", 2),
-        ("end", 4, 0),
-        ("mid", 0),
         ("far", 0),
-        ("end", 5, 0),
         ("middle", 3, 0),
         ("total", 1),
+        ("caps",),
+        ("middle", 3, 1),
+        ("end", 4, 0),
+        ("mid", 1),
         ("near", 0),
+        ("total", 3, 0),
+        ("end", 5, 0),
+        ("middle", 2),
         ("end", 4, 1),
-        ("middle", 3, 1),
-        ("total", 3, 0),
-        ("mid", 1),
         ("total", 3, 1),
-        ("middle", 2),
-        ("end", 5, 1),
-        ("mid", 3),
+        ("far", 1),
         ("finish", 0),
-        ("end", 6, 0),
-        ("far", 1),
     ),
     (
         ("middle", 4, 0),
         ("total", 2),
+        ("mid", 3),
+        ("middle", 4, 1),
+        ("end", 5, 1),
+    ),
+    (
+        ("mid", 2),
+        ("end", 6, 0),
+        ("middle", 5, 0),
+        ("near", 1),
+        ("total", 4, 1),
         ("far", 3),
-        ("near", 1),
-        ("middle", 4, 1),
-        ("mid", 2),
-        ("middle", 5, 0),
+        ("finish", 1),
+        ("far", 2),
+        ("middle", 5, 1),
+        ("end", 6, 1),
         ("total", 4, 0),
     ),
     (
-        ("middle", 5, 1),
-        ("total", 4, 1),
-        ("end", 6, 1),
+        ("total", 5, 0),
+        ("middle", 6, 0),
         ("mid", 4),
-        ("finish", 1),
+        ("total", 5, 1),
+        ("middle", 6, 1),
     ),
     (
-        ("middle", 6, 0),
-        ("total", 5, 1),
-        ("far", 2),
-        ("total", 5, 0),
-        ("near", 3),
-    ),
-    (
-        ("middle", 6, 1),
+        ("total", 6, 1),
+        ("mid", 5),
+        ("near", 2),
         ("far", 4),
         ("total", 6, 0),
-        ("total", 6, 1),
-        ("near", 2),
-        ("mid", 5),
-        ("finish", 3),
-        ("keep", 2),
         ("finish", 2),
         ("keep", 0),
         ("keep", 1),
-        ("mid", 6),
     ),
     (
+        ("mid", 6),
+        ("near", 3),
+        ("near", 4),
         ("far", 5),
     ),
     (
         ("far", 6),
-        ("near", 4),
+        ("finish", 4),
+        ("keep", 3),
+        ("finish", 3),
+        ("keep", 2),
     ),
     (
-        ("finish", 4),
-        ("keep", 3),
         ("near", 5),
     ),
     (
@@ -834,8 +834,10 @@
     hat_ref,
     slope_buf,
     active_buf,
+    wide_sem,
     load_sem,
     store_sem,
+    half_sem,
     tile_sem,
     out_sem,
     swap_send,
@@ -865,7 +867,16 @@
     def piece_rows(cell_core, cell_x, cell_y):
         return pl.ds(pl.multiple_of(((cell_core * 2 + cell_x) * 2 + cell_y) * PIECE, 16), PIECE)
 
+    def wide_load(part):
+        cols = third(part)
+        return pltpu.make_async_copy(master_hbm.at[:, cols], wide.at[:, cols], wide_sem.at[part])
+
     def swap(part):
+        wide_load(part).wait()
+        for slot in range(SLOTS):
+            master = wide[width * slot : width * (slot + 1), third(part)]
+            low[slot, :, third(part)] = master.astype(jnp.bfloat16)
+
         def send(hop, carry):
             target = lax.rem(in_plane + hop, PLANE)
             _, ty, tx, tc = place(target)
@@ -879,6 +890,9 @@
             return carry
 
         lax.fori_loop(1, PLANE, send, 0)
+        stages[part][pl.ds(2 * in_plane, 2)] = low[:, piece_rows(core, x, y), third(part)]
+        if part == 0:
+            start([load(0), load(1)])
 
     def swap_wait(part, sem):
         most = stages[part].at[pl.ds(0, 2 * PLANE - 2)]
@@ -973,8 +987,8 @@
                 )
 
     def load(at):
-        src = (x_hbm, cot_hbm, master_hbm)[at]
-        dst = (x_then_hidden, cot_then_down, wide)[at]
+        src = (x_hbm, cot_hbm)[at]
+        dst = (x_then_hidden, cot_then_down)[at]
         return pltpu.make_async_copy(src, dst, load_sem.at[at])
 
     def store(at):
@@ -982,14 +996,21 @@
             (hidden_turned, hidden_hbm),
             (ctx_ref, ctx_hbm),
             (hat_ref, hat_hbm),
-            (cot_then_down, down_hbm),
-            (mixed_ref, mixed_hbm),
-            (wide, second_hbm),
+            None,
+            None,
+            None,
             (x_turned, x_turned_hbm),
             (ctx_turned, ctx_turned_hbm),
         )[at]
-        src = src.at[pl.ds(0, 2 * ROWS)] if src is wide else src
         return pltpu.make_async_copy(src, dst, store_sem.at[at])
+
+    def half_stores(half):
+        rows = pl.ds(ROWS * half, ROWS)
+        pairs = ((cot_then_down, down_hbm), (mixed_ref, mixed_hbm), (wide, second_hbm))
+        return [
+            pltpu.make_async_copy(src.at[rows], dst.at[rows], half_sem.at[half, at])
+            for at, (src, dst) in enumerate(pairs)
+        ]
 
     def w_store(pair):
         two = pl.ds(2 * pair, 2)
@@ -1000,17 +1021,11 @@
         return value.reshape(width, value.shape[-1])
 
     def open_all():
-        for at in range(3):
-            load(at).start()
+        start([wide_load(part) for part in range(3)])
         sum_ref[...] = jnp.zeros_like(sum_ref)
         vec_ref[0:10, :] = bias_ref[...]
         vec_ref[10:12, :] = gain_ref[...]
         greet(z, in_plane)
-        load(2).wait()
-        for slot in range(SLOTS):
-            low[slot] = wide[width * slot : width * (slot + 1), :].astype(jnp.bfloat16)
-        for part in range(3):
-            stages[part][pl.ds(2 * in_plane, 2)] = low[:, piece_rows(core, x, y), third(part)]
 
     def make_caps():
         for block in range(2):
@@ -1018,7 +1033,6 @@
         load(0).wait()
         x_turned[...] = x_then_hidden[...].T
         store(6).start()
-        load(1).wait()
 
     actions = {
         "open": open_all,
@@ -1105,6 +1119,7 @@
 
     @pl.when(step == 9)
     def _():
+        load(1).wait()
         for half in range(2):
             rows = slice(ROWS * half, ROWS * half + ROWS)
             at_row = lax.broadcasted_iota(jnp.int32, (ROWS, 1), 0) + half * ROWS
@@ -1120,7 +1135,7 @@
             down_low = second.astype(jnp.bfloat16)
             cot_then_down[rows, :] = down_low
             sum_ref[7:8, :] += columns_total(down_low.astype(jnp.float32))
-        start([store(3), store(4), store(5)])
+            start(half_stores(half))
         for at in range(2):
             for copy in tile_stores(at, 0):
                 copy.wait()
@@ -1142,8 +1157,10 @@
                     z_copy(unit, part, 1).wait_send()
                     z_copy(unit, part, 2).wait_send()
 
-        for at in range(8):
+        for at in (0, 1, 2, 6, 7):
             store(at).wait()
+        for copy in half_stores(0) + half_stores(1):
+            copy.wait()
 
 
 def gathered_and_forwarded(counts, lengths, owners, bias, gain, x, cotangent, master):
@@ -1218,7 +1235,9 @@
             pltpu.VMEM((2, tokens, width), low),
             pltpu.VMEM((2, width, tokens), low),
             dma((3,)),
+            dma((2,)),
             dma((8,)),
+            dma((2, 3)),
             dma((2, 2)),
             dma((PAIRS,)),
             dma((3,)),
@@ -1247,53 +1266,52 @@
     ),
     (),
     (
+        ("core", 1),
         ("far", 0),
-        ("core", 1),
     ),
     (),
     (
+        ("core", 2),
         ("far", 1),
-        ("core", 2),
-        ("mid", 0),
     ),
     (
+        ("mid", 0),
         ("far", 2),
-    ),
-    (
-        ("end", 0),
-    ),
-    (
-        ("mid", 1),
-        ("core", 3),
     ),
     (),
     (
-        ("mid", 2),
+        ("core", 3),
+        ("mid", 1),
+        ("end", 0),
+    ),
+    (),
+    (
         ("far", 3),
         ("end", 1),
+        ("mid", 2),
+    ),
+    (
+        ("core", 4),
         ("middle", 0),
     ),
     (),
-    (),
     (
         ("middle", 1),
-        ("core", 4),
         ("end", 2),
-        ("total", 0),
         ("mid", 3),
+        ("far", 4),
     ),
     (
-        ("far", 4),
+        ("total", 0),
     ),
     (
         ("middle", 2),
         ("end", 3),
+        ("total", 1),
         ("core", 5),
-        ("total", 1),
-    ),
-    (
         ("mid", 4),
     ),
+    (),
     (
         ("far", 5),
         ("end", 4),
@@ -1305,20 +1323,20 @@
         ("core", 6),
         ("total", 3),
         ("middle", 4),
-        ("take", 0),
         ("mid", 5),
-        ("take", 1),
-        ("sum", 0),
-        ("take", 2),
         ("far", 6),
         ("total", 4),
+        ("sum", 0),
         ("end", 5),
+        ("mid", 6),
         ("middle", 5),
-        ("mid", 6),
+        ("end", 6),
+        ("take", 4),
+        ("take", 0),
         ("sum", 1),
-        ("end", 6),
+        ("take", 2),
         ("take", 3),
-        ("take", 4),
+        ("take", 1),
         ("deliver", 0),
         ("total", 5),
         ("middle", 6),
@@ -1340,10 +1358,10 @@
     q_ref,
     k_ref,
     v_ref,
-    ctx_ref,
     inverse_ref,
     gain_ref,
     late_ref,
+    ctx_hbm,
     x_turned_hbm,
     ctx_turned_hbm,
     hidden_hbm,
@@ -1361,6 +1379,7 @@
     hidden_then_x,
     active_then_ctx,
     down_then_branch,
+    ctx_ref,
     grad_ctx_ref,
     hat_ref,
     slope_then_query,
@@ -1588,6 +1607,9 @@
             None,
             (x_turned_hbm, hidden_then_x),
             (ctx_turned_hbm, active_then_ctx),
+            None,
+            None,
+            (ctx_hbm, ctx_ref),
         )[at]
         return pltpu.make_async_copy(src, dst, load_sem.at[at])
 
@@ -1626,8 +1648,7 @@
 
     @pl.when(step == 0)
     def _():
-        start([load(1), tile_load(0, 0), w_load(5), w_load(4), load(2), tile_load(0, 1), load(0)])
-        start([w_load(at) for at in range(6, TILES)] + [load(3)] + [w_load(3 - at) for at in range(4)])
+        start([load(1), tile_load(0, 0), w_load(5), w_load(4)])
         for at in range(2 * PLANE):
             tile_here, kept = jnp.int32(0), jnp.int32(0)
             for tile in range(TILES):
@@ -1659,6 +1680,23 @@
         @pl.when(step == 0)
         def _():
             load(1).wait()
+            start([load(2), tile_load(0, 1), load(0)])
+
+        @pl.when(step < 3)
+        def _():
+            start([w_load(7 + 2 * step), w_load(6 + 2 * step)])
+
+        @pl.when(step == 1)
+        def _():
+            load(3).start()
+
+        @pl.when(step == 2)
+        def _():
+            w_load(3).start()
+
+        @pl.when(step == 3)
+        def _():
+            start([load(12), w_load(0), w_load(1), w_load(2)])
 
         for half in range(2):
             rows = slice(ROWS * half, ROWS * half + ROWS)
@@ -1701,8 +1739,7 @@
     def _():
         start([load(8), load(9)])
         load(3).wait()
-        for at in range(4):
-            w_load(at).wait()
+        w_load(3).wait()
         for half in range(2):
             rows = slice(ROWS * half, ROWS * half + ROWS)
             grad_hidden, hat = acc[rows, :], hat_ref[rows, :].astype(jnp.float32)
@@ -1719,6 +1756,12 @@
 
     here = pl.ds(pl.multiple_of(block * ROWS, ROWS), ROWS)
     quad_cols = pl.ds(pl.multiple_of(quad * 256, 256), 256)
+
+    @pl.when(step == 4)
+    def _():
+        load(12).wait()
+        for at in range(3):
+            w_load(at).wait()
 
     pair_cols = pl.ds(pl.multiple_of(quad * 256 + pair * 128, 128), 128)
     grad_bufs = (slope_then_query, up_then_key, value_buf)
@@ -1795,10 +1838,10 @@
     query,
     keyed,
     valued,
-    context,
     inverse,
     gain,
     late_sums,
+    context,
     x_turned,
     ctx_turned,
     hidden,
@@ -1835,18 +1878,18 @@
         in_specs=[smem, pl.BlockSpec((1, 2, ROWS, ROWS), lambda i: (*at(i), 0, 0))]
         + [pair] * 3
         + [
-            pl.BlockSpec((tokens, width), lambda i: (0, 0), pipeline_mode=once),
             pl.BlockSpec((tokens, 1), lambda i: (0, 0), pipeline_mode=once),
             pl.BlockSpec(gain.shape, lambda i: (0, 0)),
             sums,
         ]
-        + [any_space] * 9,
+        + [any_space] * 10,
         out_specs=(any_space, any_space, sums),
         scratch_shapes=[
             pltpu.VMEM((TILES,) + cut, low),
             pltpu.VMEM((tokens, width), high),
             pltpu.VMEM((width, tokens), low),
             pltpu.VMEM((width, tokens), low),
+            pltpu.VMEM((tokens, width), low),
             pltpu.VMEM((tokens, width), low),
             pltpu.VMEM((tokens, width), low),
             pltpu.VMEM((tokens, width), low),
@@ -1866,7 +1909,7 @@
             pltpu.VMEM((6, 16, width), high),
             pltpu.SMEM((2 * PLANE,), jnp.int32),
             pltpu.SMEM((2 * PLANE,), jnp.int32),
-            dma((12,)),
+            dma((13,)),
             dma((TILES,)),
             dma((7,)),
             dma((7,)),
@@ -1891,10 +1934,10 @@
         query,
         keyed,
         valued,
-        context,
         inverse,
         gain,
         late_sums,
+        context,
         x_turned,
         ctx_turned,
         hidden,
@@ -1981,10 +2024,10 @@
             query,
             keyed,
             valued,
-            context,
             inverse,
             gain_vals,
             late_sums,
+            context,
             x_turned,
             ctx_turned,
             hidden,

time: 257 us -> 260 us (1.012)
  Pallas kernels: 255 us -> 258 us
    pallas_call x1, Pallas kernels: 19.7 us -> 22.9 us  [updated(): pl.pallas_call(functools.partial(update_kernel, gain_scale), grid=(SLOTS,...]
    pallas_call x1, Pallas kernels: 114 us -> 117 us  [gathered_and_forwarded(): pl.pallas_call(gather_and_forward, grid=(10,), out_shape=(rows, rows, row...]
where the time goes in v1:
time: 260 us; the launch traced here: 259 us
  Pallas kernels  258 us (99%)
    pallas_call x1, Pallas kernels, backward_and_reduced(): pl.pallas_call(backward_and_reduce, grid=(16,), out_shape=(shaped((tokens...  119 us
    pallas_call x1, Pallas kernels, gathered_and_forwarded(): pl.pallas_call(gather_and_forward, grid=(10,), out_shape=(rows, rows, row...  117 us
    pallas_call x1, Pallas kernels, updated(): pl.pallas_call(functools.partial(update_kernel, gain_scale), grid=(SLOTS,...  22.9 us

profile of v1, /device:TPU:11, one launch (start us, length us, event | category | flops | bytes accessed | tf_op | source)
XLA Modules:
  0.0 259.3 jit_solution(11155259291040519273)
XLA Ops:
  0.6 116.9 %gather_and_forward.1 = (bf16[1024,768]{1,0:T(8,128)(2,1)}, bf16[1024,768]{1,0:T(8,128)(2,1)}, bf16[1024,768]{1,0:T(8,128)(2,1)}, bf16[2,12,512,512]{3,2,1,0:T(8...) custom-call(s32[1,3]{1,0:T(1,128)} %counts.1, ...), custom_call_target="tpu_custom_call" | custom-call | tf_op jit(solution)/shard_map/gather_and_forward/pallas_call | solution.py:1184
  117.5 118.6 %backward_and_reduce.1 = (f32[1024,768]{1,0:T(8,128)}, bf16[2,2,2,2,96,768]{5,4,3,2,1,0:T(8,128)(2,1)}, f32[16,768]{1,0:T(8,128)}) custom-call(s32[12]{0:T(128)} %owners.3, bf16[2,12,512,512]{3,2,1,0:T(8,128)(2,1)} %get-tuple-element.42.p_ref, bf16[1024,768]{1,0:T(8,128)(2,1)} %get-tuple-element.43.q_ref, bf16[1024,768]{1,0:T(8,128)(2,1)} %get-tuple-element.44.k_ref, ...), custom_call_target="tpu_custom_call" | custom-call | tf_op jit(solution)/shard_map/backward_and_reduce/pallas_call | solution.py:1870
  236.2 22.9 %update.1 = (f32[1,2,768,768]{3,2,1,0:T(8,128)}, f32[1,2,768,768]{3,2,1,0:T(8,128)}, f32[1,2,768,768]{3,2,1,0:T(8,128)}, f32[1,2,768,768]{3,2,1,0:T(8,128)}, bf1...) custom-call(bf16[2,768,768]{2,1,0:T(8,128)(2,1)} %bitcast.3, ...), custom_call_target="tpu_custom_call" | custom-call | tf_op jit(solution)/shard_map/update/pallas_call | solution.py:588

commit v2 on v1

--- a/solution.py
+++ b/solution.py
@@ -134,20 +134,25 @@
     k_ref[...] = keyed
     v_ref[...] = valued
     low_half = lax.broadcasted_iota(jnp.int32, (1, 128), 1) < 64
-    for pair in range(2):
-        part = slice(128 * pair, 128 * pair + 128)
+
+    def attend_pair(pair, carry):
+        part = pl.ds(pl.multiple_of(128 * pair, 128), 128)
+        query, keyed, valued = q_ref[:, part], k_ref[:, part], v_ref[:, part]
         contexts = []
         for head in range(2):
             here = low_half if head == 0 else ~low_half
-            mine = jnp.where(here, query[:, part], jnp.zeros_like(query[:, part]))
-            scores = jnp.minimum(dot_back(mine, keyed[:, part]), cap_ref[...])
+            mine = jnp.where(here, query, jnp.zeros_like(query))
+            scores = jnp.minimum(dot_back(mine, keyed), cap_ref[...])
             exponent = jnp.exp(scores - jnp.max(scores, -1, keepdims=True))
             inverse = 1.0 / jnp.sum(exponent, -1, keepdims=True)
             probability = (exponent * inverse).astype(jnp.bfloat16)
             p_ref[0, 2 * pair + head] = probability
-            contexts.append(dot(probability, valued[:, part]))
+            contexts.append(dot(probability, valued))
         both = jnp.where(low_half, contexts[0], contexts[1]).astype(jnp.bfloat16)
         ctx_ref[:, pl.ds(pl.multiple_of(quad * 256 + 128 * pair, 128), 128)] = both
+        return carry
+
+    lax.fori_loop(0, 2, attend_pair, 0)
 
 
 def close_block(w_out, x_ref, vec_ref, ctx_ref, hat_ref, inverse_ref):
@@ -574,7 +579,7 @@
     input_grad,
 ):
     width = master.shape[-1]
-    chunk = 96
+    chunk = 192
     tile = pl.BlockSpec((1, 1, chunk, width), lambda s, r: (0, s, r, 0))
     steps = width // chunk
     rows = pl.BlockSpec((mixed.shape[0] // (SLOTS * steps), width), lambda s, r: (s * steps + r, 0))
@@ -1108,21 +1113,25 @@
 
     @pl.when(turn >= 0)
     def _():
-        for half in range(2):
-            rows = slice(ROWS * half, ROWS * half + ROWS)
+        def feed(half, carry):
+            rows = pl.ds(pl.multiple_of(half * ROWS, ROWS), ROWS)
             up = dot(x_then_hidden[rows, :], weight(4 + 2 * turn)) + vec_ref[pl.ds(3 + turn, 1), :]
             active, slope = gelu_parts(up)
             slope_buf[slot, rows, :] = slope.astype(jnp.bfloat16)
             active_buf[slot, :, rows] = active.T
             wide[rows, :] = wide[rows, :] + dot(active, weight(5 + 2 * turn))
+            return carry
+
+        lax.fori_loop(0, 2, feed, 0)
         start(tile_stores(slot, turn))
 
     @pl.when(step == 9)
     def _():
         load(1).wait()
-        for half in range(2):
-            rows = slice(ROWS * half, ROWS * half + ROWS)
-            at_row = lax.broadcasted_iota(jnp.int32, (ROWS, 1), 0) + half * ROWS
+
+        def close(quarter, carry):
+            rows = pl.ds(pl.multiple_of(quarter * 256, 256), 256)
+            at_row = lax.broadcasted_iota(jnp.int32, (256, 1), 0) + quarter * 256
             live = passage_facts(counts, lengths, at_row)[0].astype(jnp.float32)
             hat, inverse = normalize(wide[rows, :])
             mixed = (hat * vec_ref[11:12, :] + vec_ref[9:10, :]) * live
@@ -1135,7 +1144,12 @@
             down_low = second.astype(jnp.bfloat16)
             cot_then_down[rows, :] = down_low
             sum_ref[7:8, :] += columns_total(down_low.astype(jnp.float32))
-            start(half_stores(half))
+            return carry
+
+        lax.fori_loop(0, 2, close, 0)
+        start(half_stores(0))
+        lax.fori_loop(2, 4, close, 0)
+        start(half_stores(1))
         for at in range(2):
             for copy in tile_stores(at, 0):
                 copy.wait()
@@ -1698,12 +1712,15 @@
         def _():
             start([load(12), w_load(0), w_load(1), w_load(2)])
 
-        for half in range(2):
-            rows = slice(ROWS * half, ROWS * half + ROWS)
+        def pull(half, carry):
+            rows = pl.ds(pl.multiple_of(half * ROWS, ROWS), ROWS)
             back = dot_back(down_then_branch[rows, :], weight(5 + 2 * step))
             up_low = (back * slope_then_query[rows, :].astype(jnp.float32)).astype(jnp.bfloat16)
             up_then_key[rows, :] = up_low
             vec_now[0, pl.ds(3 + step, 1), :] += columns_total(up_low.astype(jnp.float32))
+            return carry
+
+        lax.fori_loop(0, 2, pull, 0)
 
         @pl.when(step < 3)
         def _():
@@ -1740,8 +1757,8 @@
         start([load(8), load(9)])
         load(3).wait()
         w_load(3).wait()
-        for half in range(2):
-            rows = slice(ROWS * half, ROWS * half + ROWS)
+        def open_first(quarter, carry):
+            rows = pl.ds(pl.multiple_of(quarter * 256, 256), 256)
             grad_hidden, hat = acc[rows, :], hat_ref[rows, :].astype(jnp.float32)
             vec_now[0, 10:11, :] += columns_total(grad_hidden * hat)
             vec_now[0, 8:9, :] += columns_total(grad_hidden)
@@ -1751,6 +1768,9 @@
             down_then_branch[rows, :] = branch_low
             vec_now[0, 2:3, :] += columns_total(branch_low.astype(jnp.float32))
             grad_ctx_ref[rows, :] = dot_back(branch_low, weight(3)).astype(jnp.bfloat16)
+            return carry
+
+        lax.fori_loop(0, 4, open_first, 0)
 
     serve(range(8, 20))
 

time: 260 us -> 260 us (level)
    pallas_call x1, Pallas kernels: 22.9 us -> 19.7 us  [updated(): pl.pallas_call(functools.partial(update_kernel, gain_scale), grid=(SLOTS,...]
where the time goes in v2:
time: 260 us; the launch traced here: 259 us
  Pallas kernels  258 us (99%)
    pallas_call x1, Pallas kernels, backward_and_reduced(): pl.pallas_call(backward_and_reduce, grid=(16,), out_shape=(shaped((tokens...  120 us
    pallas_call x1, Pallas kernels, gathered_and_forwarded(): pl.pallas_call(gather_and_forward, grid=(10,), out_shape=(rows, rows, row...  118 us
    pallas_call x1, Pallas kernels, updated(): pl.pallas_call(functools.partial(update_kernel, gain_scale), grid=(SLOTS,...  19.7 us

profile of v2, /device:TPU:11, one launch (start us, length us, event | category | flops | bytes accessed | tf_op | source)
XLA Modules:
  0.0 258.8 jit_solution(12968272041562101906)
XLA Ops:
  0.6 118.5 %gather_and_forward.1 = (bf16[1024,768]{1,0:T(8,128)(2,1)}, bf16[1024,768]{1,0:T(8,128)(2,1)}, bf16[1024,768]{1,0:T(8,128)(2,1)}, bf16[2,12,512,512]{3,2,1,0:T(8...) custom-call(s32[1,3]{1,0:T(1,128)} %counts.1, ...), custom_call_target="tpu_custom_call" | custom-call | tf_op jit(solution)/shard_map/gather_and_forward/pallas_call | solution.py:1198
  119.1 119.9 %backward_and_reduce.1 = (f32[1024,768]{1,0:T(8,128)}, bf16[2,2,2,2,96,768]{5,4,3,2,1,0:T(8,128)(2,1)}, f32[16,768]{1,0:T(8,128)}) custom-call(s32[12]{0:T(128)} %owners.3, bf16[2,12,512,512]{3,2,1,0:T(8,128)(2,1)} %get-tuple-element.42.p_ref, bf16[1024,768]{1,0:T(8,128)(2,1)} %get-tuple-element.43.q_ref, bf16[1024,768]{1,0:T(8,128)(2,1)} %get-tuple-element.44.k_ref, ...), custom_call_target="tpu_custom_call" | custom-call | tf_op jit(solution)/shard_map/backward_and_reduce/pallas_call | solution.py:1890
  239.0 19.7 %update.1 = (f32[1,2,768,768]{3,2,1,0:T(8,128)}, f32[1,2,768,768]{3,2,1,0:T(8,128)}, f32[1,2,768,768]{3,2,1,0:T(8,128)}, f32[1,2,768,768]{3,2,1,0:T(8,128)}, bf1...) custom-call(bf16[2,768,768]{2,1,0:T(8,128)(2,1)} %bitcast.3, ...), custom_call_target="tpu_custom_call" | custom-call | tf_op jit(solution)/shard_map/update/pallas_call | solution.py:593

commit v3 on v1

--- a/solution.py
+++ b/solution.py
@@ -518,43 +518,80 @@
     first_ref,
     second_ref,
     ema_ref,
-    vec_grad_ref,
-    bias_ref,
-    gain_ref,
-    vec_first_ref,
-    vec_second_ref,
-    vec_ema_ref,
     mixed_in,
     input_in,
+    vec_grad_hbm,
+    bias_hbm,
+    gain_hbm,
+    vec_first_hbm,
+    vec_second_hbm,
+    vec_ema_hbm,
     master_out,
     first_out,
     second_out,
     ema_out,
     copy_out,
+    mixed_out,
+    input_out,
     vec_out,
     vec_first_out,
     vec_second_out,
     vec_ema_out,
-    mixed_out,
-    input_out,
-    vec_ref,
+    vec_grad_buf,
+    bias_buf,
+    gain_buf,
+    vec_buf,
+    vec_sem,
 ):
+    step = pl.program_id(0) * pl.num_programs(1) + pl.program_id(1)
+    last = pl.num_programs(0) * pl.num_programs(1) - 1
+
+    def loads():
+        pairs = (
+            (vec_grad_hbm, vec_grad_buf),
+            (bias_hbm, bias_buf),
+            (gain_hbm, gain_buf),
+            (vec_first_hbm, vec_buf.at[1]),
+            (vec_second_hbm, vec_buf.at[2]),
+            (vec_ema_hbm, vec_buf.at[3]),
+        )
+        return [pltpu.make_async_copy(src, dst, vec_sem.at[at]) for at, (src, dst) in enumerate(pairs)]
+
+    def stores():
+        targets = (vec_out, vec_first_out, vec_second_out, vec_ema_out)
+        return [
+            pltpu.make_async_copy(vec_buf.at[at], dst, vec_sem.at[6 + at]) for at, dst in enumerate(targets)
+        ]
+
+    @pl.when(step == 0)
+    def _():
+        for load in loads():
+            load.start()
+
     mixed_out[...] = mixed_in[...]
     input_out[...] = input_in[...]
-
-    @pl.when((pl.program_id(0) == 0) & (pl.program_id(1) == 0))
-    def _():
-        vec_ref[0:10, :] = bias_ref[...]
-        vec_ref[10:12, :] = gain_ref[...]
-        vec_grad = vec_grad_ref[0:VROWS, :] * gain_scale
-        vec_out[...], vec_first_out[...], vec_second_out[...], vec_ema_out[...] = moved(
-            vec_ref[...], vec_grad, vec_first_ref[...], vec_second_ref[...], vec_ema_ref[...], vector_rate
-        )
-
     grad = grad_ref[...].astype(jnp.float32) * gain_scale
     result = moved(master_ref[0], grad, first_ref[0], second_ref[0], ema_ref[0], tile_rate)
     master_out[0], first_out[0], second_out[0], ema_out[0] = result
     copy_out[0] = result[0].astype(jnp.bfloat16)
+
+    @pl.when(step == 1)
+    def _():
+        for load in loads():
+            load.wait()
+        vec_buf[0, 0:10, :] = bias_buf[...]
+        vec_buf[0, 10:12, :] = gain_buf[...]
+        vec_grad = vec_grad_buf[0:VROWS, :] * gain_scale
+        vec_buf[0], vec_buf[1], vec_buf[2], vec_buf[3] = moved(
+            vec_buf[0], vec_grad, vec_buf[1], vec_buf[2], vec_buf[3], vector_rate
+        )
+        for store in stores():
+            store.start()
+
+    @pl.when(step == last)
+    def _():
+        for store in stores():
+            store.wait()
 
 
 def updated(
@@ -574,14 +611,11 @@
     input_grad,
 ):
     width = master.shape[-1]
-    chunk = 96
+    chunk = 192
+    steps = width // chunk
     tile = pl.BlockSpec((1, 1, chunk, width), lambda s, r: (0, s, r, 0))
-    steps = width // chunk
     rows = pl.BlockSpec((mixed.shape[0] // (SLOTS * steps), width), lambda s, r: (s * steps + r, 0))
-
-    def whole(value):
-        return pl.BlockSpec(value.shape, lambda s, r: (0, 0))
-
+    any_space = pl.BlockSpec(memory_space=pl.ANY)
     shaped = jax.ShapeDtypeStruct
     tile_shape = shaped(master.shape, jnp.float32)
     vec_shape = shaped((VROWS, width), jnp.float32)
@@ -590,14 +624,20 @@
         grid=(SLOTS, steps),
         out_shape=(tile_shape,) * 4
         + (shaped(master.shape, jnp.bfloat16),)
-        + (vec_shape,) * 4
-        + (shaped(mixed.shape, mixed.dtype), shaped(input_grad.shape, input_grad.dtype)),
+        + (shaped(mixed.shape, mixed.dtype), shaped(input_grad.shape, input_grad.dtype))
+        + (vec_shape,) * 4,
         in_specs=[pl.BlockSpec((1, chunk, width), lambda s, r: (s, r, 0))]
         + [tile] * 4
-        + [whole(value) for value in (vec_grad, bias, gain, vec_first, vec_second, vec_ema)]
-        + [rows] * 2,
-        out_specs=(tile,) * 5 + (whole(vec_first),) * 4 + (rows,) * 2,
-        scratch_shapes=[pltpu.VMEM((VROWS, width), jnp.float32)],
+        + [rows] * 2
+        + [any_space] * 6,
+        out_specs=(tile,) * 5 + (rows,) * 2 + (any_space,) * 4,
+        scratch_shapes=[
+            pltpu.VMEM(vec_grad.shape, jnp.float32),
+            pltpu.VMEM(bias.shape, jnp.float32),
+            pltpu.VMEM(gain.shape, jnp.float32),
+            pltpu.VMEM((4, VROWS, width), jnp.float32),
+            pltpu.SemaphoreType.DMA((10,)),
+        ],
         compiler_params=pltpu.CompilerParams(vmem_limit_bytes=62 * 2**20),
         name="update",
     )(
@@ -606,16 +646,16 @@
         first,
         second,
         ema,
+        mixed,
+        input_grad,
         vec_grad,
         bias,
         gain,
         vec_first,
         vec_second,
         vec_ema,
-        mixed,
-        input_grad,
     )
-    return results[-2:] + results[:-2]
+    return results[5:7] + results[:5] + results[7:]
 
 
 MESH = pl.DeviceIdType.MESH

time: 260 us -> 257 us (0.988)
    pallas_call x1, Pallas kernels: 22.9 us -> 20.3 us  [updated(): pl.pallas_call(functools.partial(update_kernel, gain_scale), grid=(SLOTS,...]
where the time goes in v3:
time: 257 us
  Pallas kernels  256 us (100%)
    pallas_call x1, Pallas kernels, backward_and_reduced(): pl.pallas_call(backward_and_reduce, grid=(16,), out_shape=(shaped((tokens...  119 us
    pallas_call x1, Pallas kernels, gathered_and_forwarded(): pl.pallas_call(gather_and_forward, grid=(10,), out_shape=(rows, rows, row...  117 us
    pallas_call x1, Pallas kernels, updated(): pl.pallas_call(functools.partial(update_kernel, gain_scale), grid=(SLOTS,...  20.3 us

profile of v3, /device:TPU:11, one launch (start us, length us, event | category | flops | bytes accessed | tf_op | source)
XLA Modules:
  0.0 256.6 jit_solution(17538663452260705412)
XLA Ops:
  0.6 116.9 %gather_and_forward.1 = (bf16[1024,768]{1,0:T(8,128)(2,1)}, bf16[1024,768]{1,0:T(8,128)(2,1)}, bf16[1024,768]{1,0:T(8,128)(2,1)}, bf16[2,12,512,512]{3,2,1,0:T(8...) custom-call(s32[1,3]{1,0:T(1,128)} %counts.1, ...), custom_call_target="tpu_custom_call" | custom-call | tf_op jit(solution)/shard_map/gather_and_forward/pallas_call | solution.py:1224
  117.5 118.6 %backward_and_reduce.1 = (f32[1024,768]{1,0:T(8,128)}, bf16[2,2,2,2,96,768]{5,4,3,2,1,0:T(8,128)(2,1)}, f32[16,768]{1,0:T(8,128)}) custom-call(s32[12]{0:T(128)} %owners.3, bf16[2,12,512,512]{3,2,1,0:T(8,128)(2,1)} %get-tuple-element.42.p_ref, bf16[1024,768]{1,0:T(8,128)(2,1)} %get-tuple-element.43.q_ref, bf16[1024,768]{1,0:T(8,128)(2,1)} %get-tuple-element.44.k_ref, ...), custom_call_target="tpu_custom_call" | custom-call | tf_op jit(solution)/shard_map/backward_and_reduce/pallas_call | solution.py:1910
  236.2 20.3 %update.1 = (f32[1,2,768,768]{3,2,1,0:T(8,128)}, f32[1,2,768,768]{3,2,1,0:T(8,128)}, f32[1,2,768,768]{3,2,1,0:T(8,128)}, f32[1,2,768,768]{3,2,1,0:T(8,128)}, bf1...) custom-call(bf16[2,768,768]{2,1,0:T(8,128)(2,1)} %bitcast.3, ...), custom_call_target="tpu_custom_call" | custom-call | tf_op jit(solution)/shard_map/update/pallas_call | solution.py:622

commit v4 on v1

--- a/solution.py
+++ b/solution.py
@@ -574,7 +574,7 @@
     input_grad,
 ):
     width = master.shape[-1]
-    chunk = 96
+    chunk = 192
     tile = pl.BlockSpec((1, 1, chunk, width), lambda s, r: (0, s, r, 0))
     steps = width // chunk
     rows = pl.BlockSpec((mixed.shape[0] // (SLOTS * steps), width), lambda s, r: (s * steps + r, 0))

time: 260 us -> 256 us (0.985)
  Pallas kernels: 258 us -> 255 us
    pallas_call x1, Pallas kernels: 22.9 us -> 19.7 us  [updated(): pl.pallas_call(functools.partial(update_kernel, gain_scale), grid=(SLOTS,...]
where the time goes in v4:
time: 256 us
  Pallas kernels  255 us (100%)
    pallas_call x1, Pallas kernels, backward_and_reduced(): pl.pallas_call(backward_and_reduce, grid=(16,), out_shape=(shaped((tokens...  119 us
    pallas_call x1, Pallas kernels, gathered_and_forwarded(): pl.pallas_call(gather_and_forward, grid=(10,), out_shape=(rows, rows, row...  117 us
    pallas_call x1, Pallas kernels, updated(): pl.pallas_call(functools.partial(update_kernel, gain_scale), grid=(SLOTS,...  19.7 us

profile of v4, /device:TPU:11, one launch (start us, length us, event | category | flops | bytes accessed | tf_op | source)
XLA Modules:
  0.0 256.0 jit_solution(17238251616981169124)
XLA Ops:
  0.6 116.9 %gather_and_forward.1 = (bf16[1024,768]{1,0:T(8,128)(2,1)}, bf16[1024,768]{1,0:T(8,128)(2,1)}, bf16[1024,768]{1,0:T(8,128)(2,1)}, bf16[2,12,512,512]{3,2,1,0:T(8...) custom-call(s32[1,3]{1,0:T(1,128)} %counts.1, ...), custom_call_target="tpu_custom_call" | custom-call | tf_op jit(solution)/shard_map/gather_and_forward/pallas_call | solution.py:1184
  117.5 118.6 %backward_and_reduce.1 = (f32[1024,768]{1,0:T(8,128)}, bf16[2,2,2,2,96,768]{5,4,3,2,1,0:T(8,128)(2,1)}, f32[16,768]{1,0:T(8,128)}) custom-call(s32[12]{0:T(128)} %owners.3, bf16[2,12,512,512]{3,2,1,0:T(8,128)(2,1)} %get-tuple-element.42.p_ref, bf16[1024,768]{1,0:T(8,128)(2,1)} %get-tuple-element.43.q_ref, bf16[1024,768]{1,0:T(8,128)(2,1)} %get-tuple-element.44.k_ref, ...), custom_call_target="tpu_custom_call" | custom-call | tf_op jit(solution)/shard_map/backward_and_reduce/pallas_call | solution.py:1870
  236.2 19.7 %update.1 = (f32[1,2,768,768]{3,2,1,0:T(8,128)}, f32[1,2,768,768]{3,2,1,0:T(8,128)}, f32[1,2,768,768]{3,2,1,0:T(8,128)}, f32[1,2,768,768]{3,2,1,0:T(8,128)}, bf1...) custom-call(bf16[2,768,768]{2,1,0:T(8,128)(2,1)} %bitcast.3, ...), custom_call_target="tpu_custom_call" | custom-call | tf_op jit(solution)/shard_map/update/pallas_call | solution.py:588
